TPU v7x, 32 devices: a whole 2x2x4 slice. The times are simulated.
32 devices in a mesh: head: 2 (over core), blk: 16 (over z, y, x).
Axes of the slice: x: 2, y: 2, z: 4, core: 2. Of those that a mesh axis runs over, the one named last changes fastest.
Arguments:
- hidden: bfloat16 [4096, 1024], P(('blk', 'head')), may hold values from -6 to 6
- adapter_index: int32 [4096], P(('blk', 'head')), may hold values from 0 to 7
- first_gain: bfloat16 [1024], P(('head', 'blk')), may hold values from 0.5 to 1.5
- first_bias: bfloat16 [1024], P(('head', 'blk')), may hold values from -1.25 to 1.25
- triple_weight: bfloat16 [1024, 3072], P(('head', 'blk')), may hold values from -0.1875 to 0.1875
- triple_bias: bfloat16 [3072], P(('head', 'blk')), may hold values from -1.25 to 1.25
- mixer_weight: bfloat16 [1024, 1024], P(('head', 'blk')), may hold values from -6 to 6
- mixer_bias: bfloat16 [1024], P(('head', 'blk')), may hold values from -1.25 to 1.25
- second_gain: bfloat16 [1024], P(('head', 'blk')), may hold values from 0.5 to 1.5
- second_bias: bfloat16 [1024], P(('head', 'blk')), may hold values from -1.25 to 1.25
- expand_weight: bfloat16 [1024, 4096], P(('head', 'blk')), may hold values from -0.1875 to 0.1875
- expand_bias: bfloat16 [4096], P(('head', 'blk')), may hold values from -1.75 to 1.75
- reduce_weight: bfloat16 [4096, 1024], P(('head', 'blk')), may hold values from -0.09375 to 0.09375
- reduce_bias: bfloat16 [1024], P(('head', 'blk')), may hold values from -1.25 to 1.25
- triple_down: bfloat16 [8, 1024, 16], replicated, may hold values from -0.1875 to 0.1875
- triple_up: bfloat16 [8, 16, 3072], replicated, may hold values from -0.75 to 0.75
- mixer_down: bfloat16 [8, 1024, 16], replicated, may hold values from -6 to 6
- mixer_up: bfloat16 [8, 16, 1024], replicated, may hold values from -0.75 to 0.75
- expand_down: bfloat16 [8, 1024, 16], replicated, may hold values from -0.1875 to 0.1875
- expand_up: bfloat16 [8, 16, 4096], replicated, may hold values from -0.75 to 0.75
- reduce_down: bfloat16 [8, 4096, 16], replicated, may hold values from -0.09375 to 0.09375
- reduce_up: bfloat16 [8, 16, 1024], replicated, may hold values from -0.75 to 0.75
- cotangent: bfloat16 [4096, 1024], P(('blk', 'head')), may hold values from -6 to 6
Outputs:
- layer_out: bfloat16 [4096, 1024], P(('blk', 'head'))
- hidden_grad: bfloat16 [4096, 1024], P(('blk', 'head'))
- triple_down_grad: float32 [8, 1024, 16], replicated
- triple_up_grad: float32 [8, 16, 3072], replicated
- mixer_down_grad: float32 [8, 1024, 16], replicated
- mixer_up_grad: float32 [8, 16, 1024], replicated
- expand_down_grad: float32 [8, 1024, 16], replicated
- expand_up_grad: float32 [8, 16, 4096], replicated
- reduce_down_grad: float32 [8, 4096, 16], replicated
- reduce_up_grad: float32 [8, 16, 1024], replicated
All inputs are finite; a program needn't handle non-finite values.
Results may differ from a plain program's by a relative error of at most 0.018.
Values may be sent and summed in bfloat16 or wider, within the bound.
A program may use at most 384 MiB of HBM per device.

v0:
```python
import math

import jax
import jax.numpy as jnp
from jax import lax
from jax.sharding import PartitionSpec as P

WIDTH = 1024
HEADS = 16
HEAD_DIM = 64
RANK = 16
ADAPTERS = 8
BLOCK = 256


EPSILON = 1e-05


def product(left, right):
    return jnp.dot(left, right, preferred_element_type=jnp.float32)


def by_transpose(left, right):
    return lax.dot_general(
        left, right, (((1,), (1,)), ((), ())), preferred_element_type=jnp.float32
    )


def transpose_by(left, right):
    return lax.dot_general(
        left, right, (((0,), (0,)), ((), ())), preferred_element_type=jnp.float32
    )


def layer_norm(stream, scales, offset):
    average = jnp.mean(stream, axis=-1, keepdims=True)
    centred = stream - average
    variance = jnp.mean(centred * centred, axis=-1, keepdims=True)
    return centred * lax.rsqrt(variance + EPSILON) * scales + offset


def selector(adapter_index):
    column = jnp.arange(ADAPTERS * RANK, dtype=jnp.int32) // RANK
    return (adapter_index[:, None] == column[None, :]).astype(jnp.float32)


def flat_down(factor):
    return jnp.transpose(factor, (1, 0, 2)).reshape(factor.shape[1], ADAPTERS * RANK)


def flat_up(factor):
    return factor.reshape(ADAPTERS * RANK, factor.shape[2])


def unflat_down(gradient):
    return jnp.transpose(gradient.reshape(gradient.shape[0], ADAPTERS, RANK), (1, 0, 2))


def unflat_up(gradient):
    return gradient.reshape(ADAPTERS, RANK, gradient.shape[1])


def projected(source, weight, offset, down_flat, up_flat, selection):
    low_rank = (selection * product(source, down_flat)).astype(jnp.bfloat16)
    return (
        product(source, weight) + offset.astype(jnp.float32) + product(low_rank, up_flat),
        low_rank,
    )


def adapter_grads(source, low_rank, out_grad, down_flat, up_flat, selection):
    rank_grad = (selection * by_transpose(out_grad, up_flat)).astype(jnp.bfloat16)
    down_grad = transpose_by(source, rank_grad)
    up_grad = transpose_by(low_rank, out_grad)
    return (down_grad, up_grad, by_transpose(rank_grad, down_flat))


def score_block(queries, keys_block):
    return jnp.einsum("qhd,khd->qhk", queries, keys_block, preferred_element_type=jnp.float32) * (
        1.0 / math.sqrt(HEAD_DIM)
    )


def cut_rows(arrays, trailing):
    length = arrays[0].shape[0]
    block_rows = math.gcd(length, 512)
    repeats = length // block_rows
    shaped = tuple(
        (
            array.reshape((repeats, block_rows) + shape_tail)
            for array, shape_tail in zip(arrays, trailing)
        )
    )
    firsts = jnp.arange(repeats, dtype=jnp.int32) * block_rows
    return (shaped, firsts, block_rows)


def forward_fold(queries, query_places, locate, totals, portion):
    head_count = queries.shape[1]
    query_block = query_places // BLOCK
    last_block = jnp.max(query_block)
    shaped, firsts, block_rows = cut_rows(portion, ((head_count, HEAD_DIM), (head_count, HEAD_DIM)))

    def forward_visiting(carried, packet):
        keys_block, values_block, first_row = packet
        key_places = locate(first_row, block_rows)

        def forward_compute(running):
            numerator, denominator = running
            allowed = (key_places // BLOCK)[None, None, :] <= query_block[:, None, None]
            powers = jnp.where(allowed, jnp.exp(score_block(queries, keys_block)), 0.0)
            numerator = numerator + jnp.einsum(
                "qhk,khd->qhd",
                powers.astype(jnp.bfloat16),
                values_block,
                preferred_element_type=jnp.float32,
            )
            return (numerator, denominator + jnp.sum(powers, axis=-1))

        skipped = jnp.min(key_places) // BLOCK > last_block
        return (lax.cond(skipped, lambda running: running, forward_compute, carried), None)

    return lax.scan(forward_visiting, totals, shaped + (firsts,))[0]


def query_grad_fold(queries, query_places, locate, numer_grad, denom_grad, totals, portion):
    head_count = queries.shape[1]
    query_block = query_places // BLOCK
    last_block = jnp.max(query_block)
    shaped, firsts, block_rows = cut_rows(portion, ((head_count, HEAD_DIM), (head_count, HEAD_DIM)))

    def query_visiting(carried, packet):
        keys_block, values_block, first_row = packet
        key_places = locate(first_row, block_rows)

        def query_compute(running):
            allowed = (key_places // BLOCK)[None, None, :] <= query_block[:, None, None]
            powers = jnp.where(allowed, jnp.exp(score_block(queries, keys_block)), 0.0)
            prob_grad = jnp.einsum(
                "qhd,khd->qhk", numer_grad, values_block, preferred_element_type=jnp.float32
            )
            score_grad = (powers * (prob_grad + denom_grad[:, :, None])).astype(jnp.bfloat16)
            return running + jnp.einsum(
                "qhk,khd->qhd", score_grad, keys_block, preferred_element_type=jnp.float32
            )

        skipped = jnp.min(key_places) // BLOCK > last_block
        return (lax.cond(skipped, lambda running: running, query_compute, carried), None)

    return lax.scan(query_visiting, totals, shaped + (firsts,))[0]


def key_grad_fold(keys_here, values_here, key_places, locate, totals, portion):
    head_count = keys_here.shape[1]
    key_block = key_places // BLOCK
    first_block = jnp.min(key_block)
    shaped, firsts, block_rows = cut_rows(
        portion, ((head_count, HEAD_DIM), (head_count, HEAD_DIM), (head_count,))
    )

    def key_visiting(carried, packet):
        query_rows, numer_rows, denom_rows, first_row = packet
        query_places = locate(first_row, block_rows)

        def key_compute(running):
            keys_grad, values_grad = running
            allowed = key_block[None, None, :] <= (query_places // BLOCK)[:, None, None]
            powers = jnp.where(allowed, jnp.exp(score_block(query_rows, keys_here)), 0.0)
            prob_grad = jnp.einsum(
                "qhd,khd->qhk", numer_rows, values_here, preferred_element_type=jnp.float32
            )
            score_grad = (powers * (prob_grad + denom_rows.astype(jnp.float32)[:, :, None])).astype(
                jnp.bfloat16
            )
            keys_grad = keys_grad + jnp.einsum(
                "qhk,qhd->khd", score_grad, query_rows, preferred_element_type=jnp.float32
            )
            values_grad = values_grad + jnp.einsum(
                "qhk,qhd->khd",
                powers.astype(jnp.bfloat16),
                numer_rows,
                preferred_element_type=jnp.float32,
            )
            return (keys_grad, values_grad)

        skipped = jnp.max(query_places) // BLOCK < first_block
        return (lax.cond(skipped, lambda running: running, key_compute, carried), None)

    return lax.scan(key_visiting, totals, shaped + (firsts,))[0]


def local(
    hidden,
    adapter_index,
    first_gain,
    first_bias,
    triple_weight,
    triple_bias,
    mixer_weight,
    mixer_bias,
    second_gain,
    second_bias,
    expand_weight,
    expand_bias,
    reduce_weight,
    reduce_bias,
    triple_down,
    triple_up,
    mixer_down,
    mixer_up,
    expand_down,
    expand_up,
    reduce_down,
    reduce_up,
    cotangent,
):
    gathered = (
        lax.all_gather(first_gain, ("head", "blk"), axis=0, tiled=True),
        lax.all_gather(first_bias, ("head", "blk"), axis=0, tiled=True),
        lax.all_gather(triple_weight, ("head", "blk"), axis=0, tiled=True),
        lax.all_gather(triple_bias, ("head", "blk"), axis=0, tiled=True),
        lax.all_gather(mixer_weight, ("head", "blk"), axis=0, tiled=True),
        lax.all_gather(mixer_bias, ("head", "blk"), axis=0, tiled=True),
        lax.all_gather(second_gain, ("head", "blk"), axis=0, tiled=True),
        lax.all_gather(second_bias, ("head", "blk"), axis=0, tiled=True),
        lax.all_gather(expand_weight, ("head", "blk"), axis=0, tiled=True),
        lax.all_gather(expand_bias, ("head", "blk"), axis=0, tiled=True),
        lax.all_gather(reduce_weight, ("head", "blk"), axis=0, tiled=True),
        lax.all_gather(reduce_bias, ("head", "blk"), axis=0, tiled=True),
    )
    (
        gain_one,
        bias_one,
        weight_triple,
        bias_triple,
        weight_mixer,
        bias_mixer,
        gain_two,
        bias_two,
        weight_expand,
        bias_expand,
        weight_reduce,
        bias_reduce,
    ) = gathered
    token_count = hidden.shape[0]
    head_ways = lax.axis_size("head")
    cycle_ways = lax.axis_size("blk")
    selection = selector(adapter_index)
    down_triple = flat_down(triple_down)
    upward_triple = flat_up(triple_up)
    down_mixer = flat_down(mixer_down)
    upward_mixer = flat_up(mixer_up)
    down_expand = flat_down(expand_down)
    upward_expand = flat_up(expand_up)
    down_reduce = flat_down(reduce_down)
    upward_reduce = flat_up(reduce_up)
    stream = hidden.astype(jnp.float32)

    def first_norm(values_in):
        return layer_norm(values_in, gain_one.astype(jnp.float32), bias_one.astype(jnp.float32))

    def second_norm(values_in):
        return layer_norm(values_in, gain_two.astype(jnp.float32), bias_two.astype(jnp.float32))

    first_normed = first_norm(stream).astype(jnp.bfloat16)
    joint, rank_triple = projected(
        first_normed, weight_triple, bias_triple, down_triple, upward_triple, selection
    )
    joint = joint.astype(jnp.bfloat16)
    parts = joint.reshape(token_count, 3, HEADS, HEAD_DIM)
    own_shard = lax.axis_index("blk") * head_ways + lax.axis_index("head")
    query_places = own_shard * token_count + jnp.arange(token_count, dtype=jnp.int32)

    def locate(first_row, length):
        rows_here = first_row + jnp.arange(length, dtype=jnp.int32)
        shard_index = rows_here // token_count
        return (
            shard_index % cycle_ways * head_ways + shard_index // cycle_ways
        ) * token_count + rows_here % token_count

    queries = parts[:, 0]
    keys_here = parts[:, 1]
    values_here = parts[:, 2]
    head_count = queries.shape[1]
    flat_keys = keys_here.reshape(token_count, head_count * HEAD_DIM)
    flat_values = values_here.reshape(token_count, head_count * HEAD_DIM)
    zeros_rows = jnp.zeros((token_count, head_count, HEAD_DIM), jnp.float32)
    payload = (flat_keys, flat_values)
    numerator, denominator = forward_fold(
        queries,
        query_places,
        locate,
        (zeros_rows, jnp.zeros((token_count, head_count), jnp.float32)),
        (
            lax.all_gather(payload[0], ("head", "blk"), axis=0, tiled=True),
            lax.all_gather(payload[1], ("head", "blk"), axis=0, tiled=True),
        ),
    )
    attended = numerator / denominator[:, :, None]
    attended_low = attended.astype(jnp.bfloat16).reshape(token_count, WIDTH)
    mixed, rank_mixer = projected(
        attended_low, weight_mixer, bias_mixer, down_mixer, upward_mixer, selection
    )
    residual = stream + mixed
    second_normed = second_norm(residual).astype(jnp.bfloat16)
    expanded, rank_expand = projected(
        second_normed, weight_expand, bias_expand, down_expand, upward_expand, selection
    )
    activated = jax.nn.gelu(expanded, approximate=True).astype(jnp.bfloat16)
    reduced, rank_reduce = projected(
        activated, weight_reduce, bias_reduce, down_reduce, upward_reduce, selection
    )
    layer_out = (residual + reduced).astype(jnp.bfloat16)
    reduce_down_grad, reduce_up_grad, through_reduce = adapter_grads(
        activated, rank_reduce, cotangent, down_reduce, upward_reduce, selection
    )
    activated_grad = (by_transpose(cotangent, weight_reduce) + through_reduce).astype(jnp.bfloat16)
    gelu_back = jax.vjp(lambda values_in: jax.nn.gelu(values_in, approximate=True), expanded)[1]
    expanded_grad = gelu_back(activated_grad.astype(jnp.float32))[0].astype(jnp.bfloat16)
    expand_down_grad, expand_up_grad, through_expand = adapter_grads(
        second_normed, rank_expand, expanded_grad, down_expand, upward_expand, selection
    )
    normed_grad = by_transpose(expanded_grad, weight_expand) + through_expand
    second_back = jax.vjp(second_norm, residual)[1]
    residual_grad = cotangent.astype(jnp.float32) + second_back(normed_grad)[0]
    mixed_grad = residual_grad.astype(jnp.bfloat16)
    mixer_down_grad, mixer_up_grad, through_mixer = adapter_grads(
        attended_low, rank_mixer, mixed_grad, down_mixer, upward_mixer, selection
    )
    attended_grad = (by_transpose(mixed_grad, weight_mixer) + through_mixer).astype(jnp.bfloat16)
    output_grad = attended_grad.reshape(token_count, HEADS, HEAD_DIM).astype(jnp.float32)
    numer_grad = (output_grad / denominator[:, :, None]).astype(jnp.bfloat16)
    denom_grad = (-jnp.sum(output_grad * attended, axis=-1) / denominator).astype(jnp.bfloat16)
    payload = (flat_keys, flat_values)
    query_grad = query_grad_fold(
        queries,
        query_places,
        locate,
        numer_grad,
        denom_grad.astype(jnp.float32),
        zeros_rows,
        (
            lax.all_gather(payload[0], ("head", "blk"), axis=0, tiled=True),
            lax.all_gather(payload[1], ("head", "blk"), axis=0, tiled=True),
        ),
    )
    payload = (
        queries.reshape(token_count, head_count * HEAD_DIM),
        numer_grad.reshape(token_count, head_count * HEAD_DIM),
        denom_grad,
    )
    keys_grad, values_grad = key_grad_fold(
        keys_here,
        values_here,
        query_places,
        locate,
        (zeros_rows, zeros_rows),
        (
            lax.all_gather(payload[0], ("head", "blk"), axis=0, tiled=True),
            lax.all_gather(payload[1], ("head", "blk"), axis=0, tiled=True),
            lax.all_gather(payload[2], ("head", "blk"), axis=0, tiled=True),
        ),
    )
    factor = 1.0 / math.sqrt(HEAD_DIM)
    joint_grad = jnp.stack([query_grad * factor, keys_grad * factor, values_grad], axis=1).astype(
        jnp.bfloat16
    )
    joint_tokens = joint_grad.reshape(token_count, 3 * WIDTH)
    triple_down_grad, triple_up_grad, through_triple = adapter_grads(
        first_normed, rank_triple, joint_tokens, down_triple, upward_triple, selection
    )
    normed_one_grad = by_transpose(joint_tokens, weight_triple) + through_triple
    first_back = jax.vjp(first_norm, stream)[1]
    hidden_grad = (residual_grad + first_back(normed_one_grad)[0]).astype(jnp.bfloat16)
    summed = lax.psum(
        (
            triple_down_grad,
            triple_up_grad,
            mixer_down_grad,
            mixer_up_grad,
            expand_down_grad,
            expand_up_grad,
            reduce_down_grad,
            reduce_up_grad,
        ),
        ("head", "blk"),
    )
    return (
        layer_out,
        hidden_grad,
        unflat_down(summed[0]),
        unflat_up(summed[1]),
        unflat_down(summed[2]),
        unflat_up(summed[3]),
        unflat_down(summed[4]),
        unflat_up(summed[5]),
        unflat_down(summed[6]),
        unflat_up(summed[7]),
    )


def solution(mesh):
    placed = (
        P(("blk", "head"), None),
        P(("blk", "head")),
        P(("head", "blk")),
        P(("head", "blk")),
        P(("head", "blk"), None),
        P(("head", "blk")),
        P(("head", "blk"), None),
        P(("head", "blk")),
        P(("head", "blk")),
        P(("head", "blk")),
        P(("head", "blk"), None),
        P(("head", "blk")),
        P(("head", "blk"), None),
        P(("head", "blk")),
        P(),
        P(),
        P(),
        P(),
        P(),
        P(),
        P(),
        P(),
        P(("blk", "head"), None),
    )
    return jax.shard_map(
        local,
        mesh=mesh,
        in_specs=placed,
        out_specs=(
            P(("blk", "head"), None),
            P(("blk", "head"), None),
            P(),
            P(),
            P(),
            P(),
            P(),
            P(),
            P(),
            P(),
        ),
        check_vma=False,
    )
```

profile of v0, /device:TPU:1, one launch (start us, length us, event | category | flops | bytes accessed | tf_op | source)
XLA Modules:
  0.0 1056.7 jit_solution(12379597912935190844)
XLA Ops:
  14.6 41.6 %all-reduce.8 = (bf16[3072]{0:T(1024)(128)(2,1)S(1)}, bf16[1024]{0:T(1024)(128)(2,1)S(1)}, bf16[1024]{0:T(1024)(128)(2,1)S(1)}, bf16[1024]{0:T(1024)(128)(2,1)S(...) all-reduce(bf16[3072]{0:T(1024)(128)(2,1)S(1)} %dynamic-update-slic, ...), channel_id=1, replica_groups=mesh['head'=2,'blk'=16] {'head','blk'}, use_global_device_ids=true, to_apply=%add.2 | all-reduce | flops 9216 | bytes 36864
  60.0 23.1 %all-gather.10.cloned.1.call-done = bf16[1024,3072]{1,0:T(8,128)(2,1)} async-done(((bf16[32,3072]{1,0:T(8,128)(2,1)}), bf16[1024,3072]{1,0:T(8,128)(2,1)}) %all-gather.10.cloned.1.call-update) | async-done | bytes 6291472 | tf_op jit(solution)/shard_map/all_gather | solution.py:220
  91.8 66.1 %all-gather = bf16[32,1,128]{2,1,0:T(2,128)(2,1)S(1)} all-gather(bf16[1,1,128]{2,1,0:T(2,128)(2,1)S(1)} %bitcast.304), channel_id=1, replica_groups=mesh['head'=2,'blk'=16] {'head','blk'}, dimensions={0}, use_global_device_ids=true | all-gather | bytes 8448 | tf_op jit(solution)/shard_map/all_gather | solution.py:227
  169.7 86.8 %all-gather.12.cloned.1.call-done = bf16[4096,1024]{0,1:T(8,128)(2,1)} async-done(((bf16[128,1024]{0,1:T(8,128)(2,1)}), bf16[4096,1024]{0,1:T(8,128)(2,1)}) %all-gather.12.cloned.1.call-update) | async-done | bytes 8388624 | tf_op jit(solution)/shard_map/all_gather | solution.py:295
  256.4 12.3 %copy.75 = bf16[128,8,8,512]{3,2,1,0:T(8,128)(2,1)} copy(bf16[128,8,8,512]{3,1,2,0:T(8,128)(2,1)} %bitcast.269) | data formatting | bytes 16777216
  278.4 71.8 %all-gather.14.cloned.1.call-done = bf16[4096,1024]{0,1:T(8,128)(2,1)} async-done(((bf16[128,1024]{0,1:T(8,128)(2,1)}), bf16[4096,1024]{0,1:T(8,128)(2,1)}) %all-gather.14.cloned.1.call-update) | async-done | bytes 8388624 | tf_op jit(solution)/shard_map/all_gather | solution.py:296
  350.2 12.7 %copy.76 = bf16[128,8,8,512]{3,2,1,0:T(8,128)(2,1)} copy(bf16[128,8,8,512]{3,1,2,0:T(8,128)(2,1)} %bitcast.270) | data formatting | bytes 16777216
  372.6 51.5 %while.49 = (s32[]{:T(128)}, f32[128,16,64]{0,2,1:T(8,128)S(1)}, f32[128,16]{0,1:T(8,128)S(1)}, s32[8]{0:T(128)S(1)}, s32[]{:T(128)}, /*index=5*/bf16[8,512,16,6...) while((s32[]{:T(128)}, f32[128,16,64]{0,2,1:T(8,128)S(1)}, ...), condition=%wide.region_8.9_spmd.clone, body=%wide.region_3.8_spmd.clone.sunk | while | flops 274956576 | bytes 12041981 | solution.py:123
  430.7 55.8 %all-gather.18.cloned.1.call-done = bf16[1024,4096]{1,0:T(8,128)(2,1)} async-done(((bf16[32,4096]{1,0:T(8,128)(2,1)}), bf16[1024,4096]{1,0:T(8,128)(2,1)}) %all-gather.18.cloned.1.call-update) | async-done | bytes 8388624 | tf_op jit(solution)/shard_map/all_gather | solution.py:226
  507.0 68.9 %all_gather.69 = bf16[4096,16]{0,1:T(8,128)(2,1)S(1)} all-gather(bf16[128,16]{0,1:T(8,128)(2,1)S(1)} %get-tuple-element.1073), channel_id=1, replica_groups=mesh['head'=2,'blk'=16] {'head','blk'}, dimensions={0}, use_global_device_ids=true | all-gather | bytes 135168 | tf_op jit(solution)/shard_map/all_gather | solution.py:361
  582.5 12.3 %copy.77 = bf16[128,8,8,512]{3,2,1,0:T(8,128)(2,1)} copy(bf16[128,8,8,512]{3,1,2,0:T(8,128)(2,1)} %bitcast.268) | data formatting | bytes 16777216
  613.1 59.8 %while.50 = (s32[]{:T(128)}, f32[128,16,64]{0,2,1:T(8,128)S(1)}, s32[8]{0:T(128)S(1)}, s32[]{:T(128)}, bf16[8,512,16,64]{1,3,2,0:T(8,128)(2,1)}, /*index=5*/bf16...) while((s32[]{:T(128)}, f32[128,16,64]{0,2,1:T(8,128)S(1)}, ...), condition=%wide.region_18.19_spmd.clone, body=%wide.region_14.18_spmd.clone.sunk | while | flops 408125728 | bytes 13263085 | solution.py:150
  673.0 22.1 %reshape.307 = bf16[8,512,16,64]{3,2,1,0:T(8,128)(2,1)} reshape(bf16[4096,1024]{1,0:T(8,128)(2,1)} %all-gather.24.cloned.1.call-done) | data formatting | bytes 16777216 | tf_op jit(solution)/shard_map/reshape | solution.py:90
  695.1 18.4 %copy.68 = bf16[8,512,16,64]{1,3,2,0:T(8,128)(2,1)} copy(bf16[8,512,16,64]{3,2,1,0:T(8,128)(2,1)} %reshape.307) | data formatting | bytes 16777216
  713.6 143.7 %while.51 = (s32[]{:T(128)}, f32[128,16,64]{0,2,1:T(8,128)S(1)}, f32[128,16,64]{0,2,1:T(8,128)S(1)}, s32[8]{0:T(128)S(1)}, s32[]{:T(128)}, /*index=5*/bf16[8,512...) while((s32[]{:T(128)}, f32[128,16,64]{0,2,1:T(8,128)S(1)}, ...), condition=%wide.region_24.25_spmd.clone, body=%wide.region_20.24_spmd.clone.sunk | while | flops 545628416 | bytes 19694368 | solution.py:189
  718.7 12.7 %conditional.11 = ((f32[128,16,64]{0,2,1:T(8,128)S(1)}, f32[128,16,64]{0,2,1:T(8,128)S(1)})) conditional(s32[]{:T(128)} %convert_element_type.326, (s32[128]{0:T(128)S(1)}, s32[512]{0:T(512)S(1)}, bf16[8,512,16,64]{1,3,2,0:T(8,128)(2,1)}, s32[]{:T(128)}, bf16[128,16,64]{0,2,1:T(8,128)(2,1)S(1)}, /*index=5*/bf16[8,512,16,64]{1,3,2,0:T(8,128)(2,1)}, ...), branch_computations={%region_22.22_spmd, %region_23.23_spmd} | conditional | flops 545604096 | bytes 19689636 | solution.py:187
  736.7 12.7 %conditional.11 = ((f32[128,16,64]{0,2,1:T(8,128)S(1)}, f32[128,16,64]{0,2,1:T(8,128)S(1)})) conditional(s32[]{:T(128)} %convert_element_type.326, (s32[128]{0:T(128)S(1)}, s32[512]{0:T(512)S(1)}, bf16[8,512,16,64]{1,3,2,0:T(8,128)(2,1)}, s32[]{:T(128)}, bf16[128,16,64]{0,2,1:T(8,128)(2,1)S(1)}, /*index=5*/bf16[8,512,16,64]{1,3,2,0:T(8,128)(2,1)}, ...), branch_computations={%region_22.22_spmd, %region_23.23_spmd} | conditional | flops 545604096 | bytes 19689636 | solution.py:187
  754.6 12.7 %conditional.11 = ((f32[128,16,64]{0,2,1:T(8,128)S(1)}, f32[128,16,64]{0,2,1:T(8,128)S(1)})) conditional(s32[]{:T(128)} %convert_element_type.326, (s32[128]{0:T(128)S(1)}, s32[512]{0:T(512)S(1)}, bf16[8,512,16,64]{1,3,2,0:T(8,128)(2,1)}, s32[]{:T(128)}, bf16[128,16,64]{0,2,1:T(8,128)(2,1)S(1)}, /*index=5*/bf16[8,512,16,64]{1,3,2,0:T(8,128)(2,1)}, ...), branch_computations={%region_22.22_spmd, %region_23.23_spmd} | conditional | flops 545604096 | bytes 19689636 | solution.py:187
  772.5 12.7 %conditional.11 = ((f32[128,16,64]{0,2,1:T(8,128)S(1)}, f32[128,16,64]{0,2,1:T(8,128)S(1)})) conditional(s32[]{:T(128)} %convert_element_type.326, (s32[128]{0:T(128)S(1)}, s32[512]{0:T(512)S(1)}, bf16[8,512,16,64]{1,3,2,0:T(8,128)(2,1)}, s32[]{:T(128)}, bf16[128,16,64]{0,2,1:T(8,128)(2,1)S(1)}, /*index=5*/bf16[8,512,16,64]{1,3,2,0:T(8,128)(2,1)}, ...), branch_computations={%region_22.22_spmd, %region_23.23_spmd} | conditional | flops 545604096 | bytes 19689636 | solution.py:187
  790.4 12.7 %conditional.11 = ((f32[128,16,64]{0,2,1:T(8,128)S(1)}, f32[128,16,64]{0,2,1:T(8,128)S(1)})) conditional(s32[]{:T(128)} %convert_element_type.326, (s32[128]{0:T(128)S(1)}, s32[512]{0:T(512)S(1)}, bf16[8,512,16,64]{1,3,2,0:T(8,128)(2,1)}, s32[]{:T(128)}, bf16[128,16,64]{0,2,1:T(8,128)(2,1)S(1)}, /*index=5*/bf16[8,512,16,64]{1,3,2,0:T(8,128)(2,1)}, ...), branch_computations={%region_22.22_spmd, %region_23.23_spmd} | conditional | flops 545604096 | bytes 19689636 | solution.py:187
  808.3 12.7 %conditional.11 = ((f32[128,16,64]{0,2,1:T(8,128)S(1)}, f32[128,16,64]{0,2,1:T(8,128)S(1)})) conditional(s32[]{:T(128)} %convert_element_type.326, (s32[128]{0:T(128)S(1)}, s32[512]{0:T(512)S(1)}, bf16[8,512,16,64]{1,3,2,0:T(8,128)(2,1)}, s32[]{:T(128)}, bf16[128,16,64]{0,2,1:T(8,128)(2,1)S(1)}, /*index=5*/bf16[8,512,16,64]{1,3,2,0:T(8,128)(2,1)}, ...), branch_computations={%region_22.22_spmd, %region_23.23_spmd} | conditional | flops 545604096 | bytes 19689636 | solution.py:187
  826.3 12.7 %conditional.11 = ((f32[128,16,64]{0,2,1:T(8,128)S(1)}, f32[128,16,64]{0,2,1:T(8,128)S(1)})) conditional(s32[]{:T(128)} %convert_element_type.326, (s32[128]{0:T(128)S(1)}, s32[512]{0:T(512)S(1)}, bf16[8,512,16,64]{1,3,2,0:T(8,128)(2,1)}, s32[]{:T(128)}, bf16[128,16,64]{0,2,1:T(8,128)(2,1)S(1)}, /*index=5*/bf16[8,512,16,64]{1,3,2,0:T(8,128)(2,1)}, ...), branch_computations={%region_22.22_spmd, %region_23.23_spmd} | conditional | flops 545604096 | bytes 19689636 | solution.py:187
  844.2 12.7 %conditional.11 = ((f32[128,16,64]{0,2,1:T(8,128)S(1)}, f32[128,16,64]{0,2,1:T(8,128)S(1)})) conditional(s32[]{:T(128)} %convert_element_type.326, (s32[128]{0:T(128)S(1)}, s32[512]{0:T(512)S(1)}, bf16[8,512,16,64]{1,3,2,0:T(8,128)(2,1)}, s32[]{:T(128)}, bf16[128,16,64]{0,2,1:T(8,128)(2,1)S(1)}, /*index=5*/bf16[8,512,16,64]{1,3,2,0:T(8,128)(2,1)}, ...), branch_computations={%region_22.22_spmd, %region_23.23_spmd} | conditional | flops 545604096 | bytes 19689636 | solution.py:187
  872.7 166.3 %all-reduce.11.cloned.1.call-done = (f32[8,1024,16]{1,2,0:T(8,128)}, f32[8,16,3072]{2,1,0:T(8,128)}, f32[8,1024,16]{1,2,0:T(8,128)}, f32[8,16,1024]{2,1,0:T(8,12...) async-done(((f32[8,1024,16]{1,2,0:T(8,128)}, f32[8,16,3072]{2,1,0:T(8,128)}, f32[8,1024,16]{1,2,0:T(8,128)}, ...) | async-done | bytes 8388624 | tf_op jit(solution)/shard_map/psum | solution.py:375
  (523 shorter events, 331.2 us)
Async XLA Ops:
  7.2 484.0 %copy-start = (bf16[8,16,4096]{2,1,0:T(8,128)(2,1)S(1)}, bf16[8,16,4096]{2,1,0:T(8,128)(2,1)}, u32[]{:S(2)}) copy-start(bf16[8,16,4096]{2,1,0:T(8,128)(2,1)} %param.54) | copy-start | bytes 3145732
  7.2 75.9 %all-gather.10.cloned.1.call-start = ((), (), s32[]{:S(2)}) async-start(), calls=%async_computation | async-start | bytes 6488064 | tf_op jit(solution)/shard_map/all_gather | solution.py:220
  7.9 154.2 %all-gather.20.cloned.1.call-start = ((), (), s32[]{:S(2)}) async-start(), calls=%async_computation.5 | async-start | bytes 8650752 | tf_op jit(solution)/shard_map/all_gather | solution.py:228
  8.7 247.8 %all-gather.12.cloned.1.call-start = ((), (), s32[]{:S(2)}) async-start(), calls=%async_computation.1 | async-start | bytes 8650752 | tf_op jit(solution)/shard_map/all_gather | solution.py:295
  56.2 443.8 %copy-start.62 = (s32[128]{0:T(128)}, s32[128]{0:T(128)S(1)}, u32[]{:S(2)}) copy-start(s32[128]{0:T(128)S(1)} %and_select_fusion) | copy-start | bytes 1540
  58.5 28.6 %copy-start.71 = (f32[128]{0:T(128)}, f32[128]{0:T(128)S(1)}, u32[]{:S(2)}) copy-start(f32[128]{0:T(128)S(1)} %fusion.142) | copy-start | bytes 1540
  58.5 28.6 %copy-start.65 = (f32[128]{0:T(128)}, f32[128]{0:T(128)S(1)}, u32[]{:S(2)}) copy-start(f32[128]{0:T(128)S(1)} %fusion.151) | copy-start | bytes 1540
  87.1 71.5 %copy-start.15 = (bf16[128,1024]{1,0:T(8,128)(2,1)S(1)}, bf16[128,1024]{1,0:T(8,128)(2,1)}, u32[]{:S(2)}) copy-start(bf16[128,1024]{1,0:T(8,128)(2,1)} %param.57) | copy-start | bytes 786436
  87.2 71.5 %copy-start.61 = (s32[128]{0:T(128)S(1)}, s32[128]{0:T(128)}, u32[]{:S(2)}) copy-start(s32[128]{0:T(128)} %param.36) | copy-start | bytes 1540
  89.2 261.0 %all-gather.14.cloned.1.call-start = ((), (), s32[]{:S(2)}) async-start(), calls=%async_computation.2 | async-start | bytes 8650752 | tf_op jit(solution)/shard_map/all_gather | solution.py:296
  89.8 335.8 %all-gather.16.cloned.1.call-start = ((), (), s32[]{:S(2)}) async-start(), calls=%async_computation.3 | async-start | bytes 2162688 | tf_op jit(solution)/shard_map/all_gather | solution.py:222
  90.4 396.1 %all-gather.18.cloned.1.call-start = ((), (), s32[]{:S(2)}) async-start(), calls=%async_computation.4 | async-start | bytes 8650752 | tf_op jit(solution)/shard_map/all_gather | solution.py:226
  91.0 491.6 %all-gather.22.cloned.1.call-start = ((), (), s32[]{:S(2)}) async-start(), calls=%async_computation.6 | async-start | bytes 8650752 | tf_op jit(solution)/shard_map/all_gather | solution.py:359
  91.7 581.2 %all-gather.24.cloned.1.call-start = ((), (), s32[]{:S(2)}) async-start(), calls=%async_computation.7 | async-start | bytes 8650752 | tf_op jit(solution)/shard_map/all_gather | solution.py:360
  159.8 332.3 %copy-start.59 = (bf16[128,128]{1,0:T(8,128)(2,1)}, bf16[128,128]{1,0:T(8,128)(2,1)S(1)}, u32[]{:S(2)}) copy-start(bf16[128,128]{1,0:T(8,128)(2,1)S(1)} %fusion.136) | copy-start | bytes 98308
  372.6 52.7 %copy-start.38 = (bf16[8,1024,16]{1,2,0:T(8,128)(2,1)S(1)}, bf16[8,1024,16]{1,2,0:T(8,128)(2,1)}, u32[]{:S(2)}) copy-start(bf16[8,1024,16]{1,2,0:T(8,128)(2,1)} %param.51) | copy-start | bytes 786436
  429.0 70.6 %copy-start.5 = (f32[128,1024]{1,0:T(8,128)}, f32[128,1024]{1,0:T(8,128)S(1)}, u32[]{:S(2)}) copy-start(f32[128,1024]{1,0:T(8,128)S(1)} %get-tuple-element.1099) | copy-start | bytes 1572868
  429.4 61.7 %copy-start.19 = (bf16[128,1024]{1,0:T(8,128)(2,1)}, bf16[128,1024]{1,0:T(8,128)(2,1)S(1)}, u32[]{:S(2)}) copy-start(bf16[128,1024]{1,0:T(8,128)(2,1)S(1)} %add_convert_fusion.1) | copy-start | bytes 786436
  430.7 60.5 %copy-start.44 = (bf16[128,128]{1,0:T(8,128)(2,1)}, bf16[128,128]{1,0:T(8,128)(2,1)S(1)}, u32[]{:S(2)}) copy-start(bf16[128,128]{1,0:T(8,128)(2,1)S(1)} %fusion.135) | copy-start | bytes 98308
  492.2 119.1 %copy-start.2 = (bf16[128,4096]{1,0:T(8,128)(2,1)}, bf16[128,4096]{1,0:T(8,128)(2,1)S(1)}, u32[]{:S(2)}) copy-start(bf16[128,4096]{1,0:T(8,128)(2,1)S(1)} %get-tuple-element.1100) | copy-start | bytes 3145732
  500.2 75.8 %copy-start.25 = (bf16[128,1024]{1,0:T(8,128)(2,1)}, bf16[128,1024]{1,0:T(8,128)(2,1)S(1)}, u32[]{:S(2)}) copy-start(bf16[128,1024]{1,0:T(8,128)(2,1)S(1)} %fusion.147) | copy-start | bytes 786436
  501.0 93.9 %copy-start.50 = (bf16[128,128]{1,0:T(8,128)(2,1)}, bf16[128,128]{1,0:T(8,128)(2,1)S(1)}, u32[]{:S(2)}) copy-start(bf16[128,128]{1,0:T(8,128)(2,1)S(1)} %fusion.137) | copy-start | bytes 98308
  502.8 536.2 %all-reduce.11.cloned.1.call-start = ((), (), s32[]{:S(2)}) async-start(), calls=%async_computation.8 | async-start | bytes 16777216 | tf_op jit(solution)/shard_map/psum | solution.py:375
  713.6 144.0 %copy-start.58 = (bf16[128,128]{1,0:T(8,128)(2,1)S(1)}, bf16[128,128]{1,0:T(8,128)(2,1)}, u32[]{:S(2)}) copy-start(bf16[128,128]{1,0:T(8,128)(2,1)} %copy-done.57) | copy-start | bytes 98308
  (65 other events, 391.1 us)
Sparse Core Ops, SparseCore 0:
  10.9 72.1 all-gather.9
  86.0 76.0 all-gather.19
  165.5 90.8 all-gather.11
  259.7 90.4 all-gather.13
  352.9 54.5 all-gather.15
  410.2 76.1 all-gather.17
  489.9 92.6 all-gather.21
  585.4 75.4 all-gather.23
  860.8 178.2 all-reduce.10
where the time goes:
time: 1070 us; the launch traced here: 1060 us
  waiting for transfers between devices  416 us (39%)
  matrix products  181 us (17%)
  blocking collectives  177 us (17%)
  local copies, waits for them, and re-layouts  145 us (14%)
  loops' own time  79.8 us (7%)
  other arithmetic  42 us (4%)
  between operations  15.6 us (1%)
    psum x1, waiting for transfers between devices, local(): lax.psum((triple_down_grad, triple_up_grad, mixer_down_grad, mixer_up_gra...  166 us
    unnamed x189, local copies, waits for them, and re-layouts  105 us
    all_gather x2, waiting for transfers between devices, local(): lax.all_gather(payload[0], ('head', 'blk'), axis=0, tiled=True)  93.4 us
    all_gather x2, waiting for transfers between devices, local(): lax.all_gather(payload[1], ('head', 'blk'), axis=0, tiled=True)  71.8 us
    all_gather x1, blocking collectives, local(): lax.all_gather(payload[2], ('head', 'blk'), axis=0, tiled=True)  68.9 us
    all_gather x1, blocking collectives, local(): lax.all_gather(expand_bias, ('head', 'blk'), axis=0, tiled=True)  66.1 us
    all_gather x1, waiting for transfers between devices, local(): lax.all_gather(expand_weight, ('head', 'blk'), axis=0, tiled=True)  55.8 us
    dot_general x12, matrix products, score_block(): jnp.einsum('qhd,khd->qhk', queries, keys_block, preferred_element_type=jn...  46.1 us
  transfers between devices with their start and end apart: 9, of which 7 were waited for; matrix products, arithmetic and copies ran while one was open for 18% of the time, Pallas kernels for 0%

commit v1 on v0

--- a/solution.py
+++ b/solution.py
@@ -1,8 +1,11 @@
+import functools
 import math
 
 import jax
 import jax.numpy as jnp
 from jax import lax
+from jax.experimental import pallas as pl
+from jax.experimental.pallas import tpu as pltpu
 from jax.sharding import PartitionSpec as P
 
 WIDTH = 1024
@@ -399,6 +402,619 @@
     )
 
 
+MESH = pl.DeviceIdType.MESH
+CHIPS = 16
+ROWS = 128
+LIMIT = 60 * 1024 * 1024
+
+
+class Links:
+    def __init__(self):
+        self.h = lax.axis_index("head")
+        self.b = lax.axis_index("blk")
+        self.o = 1 - self.h
+        self.sent = []
+        x = lax.rem(self.b, 2)
+        y = lax.rem(self.b // 2, 2)
+        self.xb = self.b + 1 - 2 * x
+        self.yb = self.b + 2 - 4 * y
+        self.db = self.xb + 2 - 4 * y
+
+    def ahead(self, k):
+        return lax.rem(self.b + k, CHIPS)
+
+    def behind(self, k):
+        return lax.rem(self.b + CHIPS - k, CHIPS)
+
+    def greet(self):
+        barrier = pltpu.get_barrier_semaphore()
+        for k in range(1, CHIPS):
+            pl.semaphore_signal(
+                barrier, 1, device_id=(self.h, self.ahead(k)), device_id_type=MESH
+            )
+        pl.semaphore_signal(barrier, 1, device_id=(self.o, self.b), device_id_type=MESH)
+        pl.semaphore_wait(barrier, CHIPS)
+
+    def send(self, source, target, send_sem, recv_sem, device):
+        copy = pltpu.make_async_remote_copy(
+            src_ref=source,
+            dst_ref=target,
+            send_sem=send_sem,
+            recv_sem=recv_sem,
+            device_id=device,
+            device_id_type=MESH,
+        )
+        copy.start()
+        self.sent.append(copy)
+        return copy
+
+    def arrived(self, target, send_sem, recv_sem):
+        pltpu.make_async_remote_copy(
+            src_ref=target,
+            dst_ref=target,
+            send_sem=send_sem,
+            recv_sem=recv_sem,
+            device_id=(self.o, self.b),
+            device_id_type=MESH,
+        ).wait_recv()
+
+    def settle(self):
+        for copy in self.sent:
+            copy.wait_send()
+        self.sent = []
+
+
+def half_mask(rows):
+    return lax.broadcasted_iota(jnp.int32, (rows, 128), 1) < 64
+
+
+def swap(tile):
+    return pltpu.roll(tile, 64, 1)
+
+
+def rows_at(ref, start, count):
+    return ref.at[pl.ds(pl.multiple_of(start, 16), count), :]
+
+
+class Gather:
+    def __init__(self, links, number, slot, sems):
+        self.links, self.p, self.slot = links, number, slot
+        self.sems = sems
+
+    def start(self):
+        l = self.links
+        self.own(0, l.b)
+        return self
+
+    def line(self, k):
+        (zs, zr) = self.sems["z"]
+        l = self.links
+        piece = self.slot(l.h, l.b)
+        l.send(piece, piece, zs.at[self.p, k], zr.at[self.p, k], (l.h, l.ahead(4 * k)))
+
+    def own(self, j, chip):
+        l = self.links
+        piece = self.slot(l.h, chip)
+        (xs, xr), (ys, yr) = (self.sems["x"], self.sems["y"])
+        l.send(piece, piece, xs.at[self.p, j], xr.at[self.p, j], (l.h, l.xb))
+        l.send(piece, piece, ys.at[self.p, j], yr.at[self.p, j], (l.h, l.yb))
+        if j == 0:
+            for k in range(1, 4):
+                self.line(k)
+        self.other(j, chip)
+
+    def other(self, number, chip):
+        l = self.links
+        piece = self.slot(l.h, chip)
+        (cs, cr) = self.sems["c"]
+        l.send(piece, piece, cs.at[self.p, number], cr.at[self.p, number], (l.o, l.b))
+
+    def from_line(self, j):
+        l = self.links
+        chip = l.behind(4 * j)
+        (s, r) = self.sems["z"]
+        l.arrived(self.slot(l.h, chip), s.at[self.p, j], r.at[self.p, j])
+        self.own(j, chip)
+
+    def shifted(self, base, j):
+        return lax.rem(base + CHIPS - 4 * j, CHIPS)
+
+    def from_side(self, axis, j):
+        l = self.links
+        chip = self.shifted(l.xb if axis == "x" else l.yb, j)
+        (s, r) = self.sems[axis]
+        piece = self.slot(l.h, chip)
+        l.arrived(piece, s.at[self.p, j], r.at[self.p, j])
+        if (j % 2 == 0) == (axis == "x"):
+            (ds, dr) = self.sems["d"]
+            target = l.yb if axis == "x" else l.xb
+            l.send(piece, piece, ds.at[self.p, j], dr.at[self.p, j], (l.h, target))
+        self.other((4 if axis == "x" else 8) + j, chip)
+
+    def from_corner(self, j):
+        l = self.links
+        chip = self.shifted(l.db, j)
+        (s, r) = self.sems["d"]
+        l.arrived(self.slot(l.h, chip), s.at[self.p, j], r.at[self.p, j])
+        self.other(12 + j, chip)
+
+    def events(self):
+        found = [self.start]
+        for j in range(4):
+            if j:
+                found.append(functools.partial(self.from_line, j))
+            found.append(functools.partial(self.from_side, "x", j))
+            found.append(functools.partial(self.from_side, "y", j))
+        for j in range(4):
+            found.append(functools.partial(self.from_corner, j))
+        return found
+
+    def whole(self):
+        l = self.links
+        (s, r) = self.sems["c"]
+        bases = (l.b, l.xb, l.yb, l.db)
+        for number in range(16):
+            chip = self.shifted(bases[number // 4], number % 4)
+            l.arrived(self.slot(l.o, chip), s.at[self.p, number], r.at[self.p, number])
+
+
+def shard_of(h, chip):
+    return h * CHIPS + chip
+
+
+def normalise(stream, gain, bias):
+    average = jnp.mean(stream, axis=-1, keepdims=True)
+    centred = stream - average
+    variance = jnp.mean(centred * centred, axis=-1, keepdims=True)
+    return centred * lax.rsqrt(variance + EPSILON) * gain + bias
+
+
+PIECES = 13
+
+
+def front_kernel(
+    hidden, sel, small_sh, triple_sh, mixer_sh, reduce_sh, expand_sh, down_t, up_t,
+    wt, wm, wr, we, vecs, bias_e, first_normed, rank_triple, kv, q, attden, attended,
+    small, bias_t, send_kv, send_q, recv_q, ones_v, send_a, recv_a,
+    lsem, zs, zr, xs, xr, ys, yr, ds, dr, cs, cr, ks, kr, qs, qr, fs, fr, as_, ar,
+):
+    l = Links()
+    mine = shard_of(l.h, l.b)
+    local_copies = [
+        pltpu.make_async_copy(small_sh, rows_at(small, mine * 16, 16), lsem.at[0]),
+        pltpu.make_async_copy(triple_sh, rows_at(wt, mine * 32, 32), lsem.at[1]),
+        pltpu.make_async_copy(mixer_sh, rows_at(wm, mine * 32, 32), lsem.at[2]),
+        pltpu.make_async_copy(reduce_sh, rows_at(wr, mine * 128, 128), lsem.at[3]),
+        pltpu.make_async_copy(expand_sh, rows_at(we, mine * 32, 32), lsem.at[4]),
+    ]
+    for copy in local_copies:
+        copy.start()
+    l.greet()
+    for copy in local_copies:
+        copy.wait()
+    sems = {"z": (zs, zr), "x": (xs, xr), "y": (ys, yr), "d": (ds, dr), "c": (cs, cr)}
+
+    def columns(ref, at):
+        return lambda h, chip: ref.at[
+            pl.ds(pl.multiple_of(shard_of(h, chip) * 32, 32), 32), at : at + 1024
+        ]
+
+    def inner(ref, at):
+        return lambda h, chip: ref.at[
+            pl.ds(pl.multiple_of(shard_of(h, chip) * 128 + at, 32), 32), :
+        ]
+
+    slots = [lambda h, chip: rows_at(small, shard_of(h, chip) * 16, 16)]
+    slots += [columns(wt, m * 1024) for m in range(3)]
+    slots += [columns(wm, 0)]
+    slots += [inner(wr, m * 32) for m in range(4)]
+    slots += [columns(we, m * 1024) for m in range(4)]
+    pieces = [Gather(l, n, slot, sems) for n, slot in enumerate(slots)]
+    for piece in pieces[:4]:
+        for event in piece.events():
+            event()
+    waiting = []
+    for piece in pieces[4:]:
+        waiting += piece.events()
+
+    def pump(count):
+        for _ in range(min(count, len(waiting))):
+            waiting.pop(0)()
+
+    waiting.pop(0)()
+    pieces[0].whole()
+    for g in range(8):
+        tile = jnp.zeros((16, 128), jnp.float32)
+        for n in range(4):
+            at = (4 * g + n) * 16
+            tile = tile + small[at : at + 16, :].astype(jnp.float32)
+        vecs[:, g * 128 : (g + 1) * 128] = tile
+        for n in range(3):
+            at = (g * 3 + n) * 128
+            bias_t[0:1, at : at + 128] = tile[6 + n : 7 + n, :]
+        for n in range(4):
+            at = (g * 4 + n) * 128
+            bias_e[0:1, at : at + 128] = tile[9 + n : 10 + n, :]
+    normed = normalise(hidden[...].astype(jnp.float32), vecs[0:1, :], vecs[1:2, :])
+    first_normed[...] = normed.astype(jnp.bfloat16)
+    rank_triple[...] = (sel[...] * by_transpose(first_normed[...], down_t[...])).astype(
+        jnp.bfloat16
+    )
+    for piece in pieces[1:4]:
+        piece.whole()
+    low = half_mask(128)
+    low64 = half_mask(64)
+    for step in range(4):
+
+        def joint(part):
+            at = part * 1024 + step * 256
+            tile = (
+                product(first_normed[...], wt[:, at : at + 256])
+                + bias_t[0:1, at : at + 256]
+                + product(rank_triple[...], up_t[:, at : at + 256])
+            )
+            return tile[:, :128], tile[:, 128:]
+
+        for n, (qt, kt, vt) in enumerate(zip(joint(0), joint(1), joint(2))):
+            c = step * 4 + n * 2
+            bf = jnp.bfloat16
+            send_kv[c * 128 : c * 128 + 128, :] = jnp.where(low, kt, swap(vt)).astype(bf)
+            send_kv[c * 128 + 128 : c * 128 + 256, :] = jnp.where(low, swap(kt), vt).astype(bf)
+            qt = qt.astype(bf).astype(jnp.float32) * 0.125
+            turned = swap(qt)
+            send_q[c * 64 : c * 64 + 64, :] = jnp.where(low64, qt[:64], turned[64:]).astype(bf)
+            send_q[c * 64 + 64 : c * 64 + 128, :] = jnp.where(
+                low64, turned[:64], qt[64:]
+            ).astype(bf)
+    own = l.b * 256 + l.h * 128
+
+    def kv_at(chip, h):
+        return rows_at(kv, chip * 256 + h * 128, 128)
+
+    for k in range(1, CHIPS):
+        t = l.ahead(k)
+        l.send(rows_at(send_kv, t * 128, 128), kv_at(l.b, l.h), ks.at[k], kr.at[k], (l.h, t))
+    for k in range(1, CHIPS):
+        t = l.ahead(k)
+        l.send(rows_at(send_q, t * 64, 64), rows_at(recv_q, l.b * 64, 64), qs.at[k], qr.at[k], (l.h, t))
+    kv[pl.ds(pl.multiple_of(own, 128), 128), :] = send_kv[pl.ds(pl.multiple_of(l.b * 128, 128), 128), :]
+    recv_q[pl.ds(pl.multiple_of(l.b * 64, 64), 64), :] = send_q[pl.ds(pl.multiple_of(l.b * 64, 64), 64), :]
+    l.send(kv_at(l.b, l.h), kv_at(l.b, l.h), fs.at[0], fr.at[0], (l.o, l.b))
+    for k in range(1, CHIPS):
+        c = l.behind(k)
+        l.arrived(kv_at(c, l.h), ks.at[k], kr.at[k])
+        l.send(kv_at(c, l.h), kv_at(c, l.h), fs.at[k], fr.at[k], (l.o, l.b))
+        pump(2)
+    for k in range(1, CHIPS):
+        l.arrived(rows_at(recv_q, l.behind(k) * 64, 64), qs.at[k], qr.at[k])
+        pump(1)
+    for k in range(CHIPS):
+        l.arrived(kv_at(l.behind(k), l.o), fs.at[k], fr.at[k])
+    for n in range(CHIPS):
+        tile = recv_q[n * 64 : n * 64 + 64, :].astype(jnp.float32)
+        q[n * 128 : n * 128 + 64, :] = jnp.where(low64, tile, 0.0).astype(jnp.bfloat16)
+        q[n * 128 + 64 : n * 128 + 128, :] = jnp.where(low64, swap(tile), 0.0).astype(jnp.bfloat16)
+        tile = kv[n * 256 : n * 256 + 256, :].astype(jnp.float32)
+        ones_v[n * 256 : n * 256 + 256, :] = jnp.where(half_mask(256), 1.0, tile).astype(jnp.bfloat16)
+    for i in range(8):
+        queries = q[i * 256 : (i + 1) * 256, :]
+
+        def fold(jj, total, masked=False):
+            at = pl.ds(pl.multiple_of(jj * 512, 512), 512)
+            powers = jnp.exp(by_transpose(queries, kv[at, :]))
+            if masked:
+                row = lax.broadcasted_iota(jnp.int32, (256, 512), 0)
+                column = lax.broadcasted_iota(jnp.int32, (256, 512), 1)
+                powers = jnp.where((row >= 128) | (column < 256), powers, 0.0)
+            return total + product(powers.astype(jnp.bfloat16), ones_v[at, :])
+
+        total = fold(i, jnp.zeros((256, 128), jnp.float32), True)
+        if i:
+            total = lax.fori_loop(0, i, fold, total)
+        share = total / swap(total)
+        attden[i * 256 : (i + 1) * 256, :] = jnp.where(half_mask(256), total, share)
+        for n in range(2):
+            t = 2 * i + n
+            part = share[n * 128 : n * 128 + 128]
+            packed = jnp.where(low64, swap(part[64:]), part[:64]).astype(jnp.bfloat16)
+            send_a[t * 64 : t * 64 + 64, :] = packed
+        pump(10)
+    for k in range(1, CHIPS):
+        t = l.ahead(k)
+        l.send(rows_at(send_a, t * 64, 64), rows_at(recv_a, l.b * 64, 64), as_.at[k], ar.at[k], (l.h, t))
+    recv_a[pl.ds(pl.multiple_of(l.b * 64, 64), 64), :] = send_a[pl.ds(pl.multiple_of(l.b * 64, 64), 64), :]
+    pump(1000)
+    for k in range(1, CHIPS):
+        l.arrived(rows_at(recv_a, l.behind(k) * 64, 64), as_.at[k], ar.at[k])
+    for p in range(8):
+        one = recv_a[p * 128 : p * 128 + 64, :].astype(jnp.float32)
+        two = recv_a[p * 128 + 64 : p * 128 + 128, :].astype(jnp.float32)
+        at = p * 128
+        attended[0:64, at : at + 128] = jnp.where(low64, swap(one), two).astype(jnp.bfloat16)
+        attended[64:128, at : at + 128] = jnp.where(low64, one, swap(two)).astype(jnp.bfloat16)
+    for piece in pieces[4:]:
+        piece.whole()
+    l.settle()
+
+
+def front(hidden, sel, small_sh, triple_sh, mixer_sh, reduce_sh, expand_sh, down_t, up_t):
+    bf, f4 = jnp.bfloat16, jnp.float32
+    vmem = pl.BlockSpec(memory_space=pltpu.VMEM)
+    hbm = pl.BlockSpec(memory_space=pl.ANY)
+    shape = jax.ShapeDtypeStruct
+    dma = pltpu.SemaphoreType.DMA
+    return pl.pallas_call(
+        front_kernel,
+        name="front",
+        in_specs=[vmem, vmem, hbm, hbm, hbm, hbm, hbm, vmem, vmem],
+        out_shape=[
+            shape((1024, 3072), bf),
+            shape((1024, 1024), bf),
+            shape((4096, 1024), bf),
+            shape((1024, 4096), bf),
+            shape((16, 1024), f4),
+            shape((1, 4096), f4),
+            shape((128, 1024), bf),
+            shape((128, 128), bf),
+            shape((4096, 128), bf),
+            shape((2048, 128), bf),
+            shape((2048, 128), f4),
+            shape((128, 1024), bf),
+        ],
+        out_specs=[vmem] * 12,
+        scratch_shapes=[
+            pltpu.VMEM((512, 128), bf),
+            pltpu.VMEM((1, 3072), f4),
+            pltpu.VMEM((2048, 128), bf),
+            pltpu.VMEM((1024, 128), bf),
+            pltpu.VMEM((1024, 128), bf),
+            pltpu.VMEM((4096, 128), bf),
+            pltpu.VMEM((1024, 128), bf),
+            pltpu.VMEM((1024, 128), bf),
+            dma((5,)),
+            dma((PIECES, 4)), dma((PIECES, 4)),
+            dma((PIECES, 4)), dma((PIECES, 4)),
+            dma((PIECES, 4)), dma((PIECES, 4)),
+            dma((PIECES, 4)), dma((PIECES, 4)),
+            dma((PIECES, 16)), dma((PIECES, 16)),
+            dma((16,)), dma((16,)),
+            dma((16,)), dma((16,)),
+            dma((16,)), dma((16,)),
+            dma((16,)), dma((16,)),
+        ],
+        compiler_params=pltpu.CompilerParams(
+            collective_id=0, has_side_effects=True, vmem_limit_bytes=LIMIT
+        ),
+    )(hidden, sel, small_sh, triple_sh, mixer_sh, reduce_sh, expand_sh, down_t, up_t)
+
+
+def back_kernel(
+    kv, q, attden, agrad,
+    joint_grad,
+    send_g, recv_g, qd, qz, dz, kz, vz, k_t, ddrow, dq_t, part, recv_part, send_kv, send_q, recv_kv, recv_q,
+    gs, gr, es, er, ks, kr, qs, qr,
+):
+    bf, f4 = jnp.bfloat16, jnp.float32
+    l = Links()
+    low, low64 = half_mask(128), half_mask(64)
+    l.greet()
+    for p in range(8):
+        tile = agrad[:, p * 128 : (p + 1) * 128].astype(f4)
+        turned = swap(tile)
+        send_g[p * 128 : p * 128 + 64, :] = jnp.where(low64, tile[64:], turned[:64]).astype(bf)
+        send_g[p * 128 + 64 : p * 128 + 128, :] = jnp.where(low64, turned[64:], tile[:64]).astype(bf)
+    for k in range(1, CHIPS):
+        t = l.ahead(k)
+        l.send(rows_at(send_g, t * 64, 64), rows_at(recv_g, l.b * 64, 64), gs.at[k], gr.at[k], (l.h, t))
+    recv_g[pl.ds(pl.multiple_of(l.b * 64, 64), 64), :] = send_g[pl.ds(pl.multiple_of(l.b * 64, 64), 64), :]
+    for n in range(CHIPS):
+        tile = kv[n * 256 : n * 256 + 256, :].astype(f4)
+        wide = half_mask(256)
+        kz[n * 256 : n * 256 + 256, :] = jnp.where(wide, tile, 0.0).astype(bf)
+        vz[n * 256 : n * 256 + 256, :] = jnp.where(wide, 0.0, tile).astype(bf)
+        k_t[:, n * 256 : n * 256 + 256] = tile.T[:64, :].astype(bf)
+    dq_t[...] = jnp.zeros_like(dq_t)
+    for k in range(1, CHIPS):
+        l.arrived(rows_at(recv_g, l.behind(k) * 64, 64), gs.at[k], gr.at[k])
+    for n in range(CHIPS):
+        at = n * 128
+        g = recv_g[n * 64 : n * 64 + 64, :].astype(f4)
+        both = attden[at : at + 128, :]
+        grad = jnp.concatenate([g, swap(g)], axis=0)
+        numer = jnp.where(low, 0.0, grad / swap(both))
+        numer_low = numer.astype(bf)
+        dz[at : at + 128, :] = numer_low
+        held = q[at : at + 128, :]
+        qz[at : at + 128, :] = held
+        qd[at : at + 128, :] = jnp.where(low, held.astype(f4), numer_low.astype(f4)).astype(bf)
+        term = jnp.where(low, 0.0, numer * both)
+        row = -jnp.sum(term.T, axis=0, keepdims=True)
+        ddrow[0:1, at : at + 128] = row.astype(bf).astype(f4)
+
+    def exchange(jj):
+        for n in range(2):
+            t = 2 * jj + n
+            l.send(
+                rows_at(part, t * 256 + l.o * 128, 128), rows_at(recv_part, t * 128, 128),
+                es.at[t], er.at[t], (l.o, l.b),
+            )
+
+    def finish(jj):
+        for n in range(2):
+            t = 2 * jj + n
+            l.arrived(rows_at(recv_part, t * 128, 128), es.at[t], er.at[t])
+            here = part[pl.ds(pl.multiple_of(t * 256 + l.h * 128, 128), 128), :]
+            send_kv[t * 128 : t * 128 + 128, :] = (here + recv_part[t * 128 : t * 128 + 128, :]).astype(bf)
+            y = dq_t[:, t * 128 : t * 128 + 128].T * 0.125
+            send_q[t * 64 : t * 64 + 64, :] = jnp.where(low64, y[:64], swap(y[64:])).astype(bf)
+
+    for jj in range(8):
+        keys = slice(jj * 512, jj * 512 + 512)
+
+        def fold(i, total, masked=False):
+            at = pl.ds(pl.multiple_of(i * 256, 256), 256)
+            both = qd[at, :]
+            powers = jnp.exp(by_transpose(kz[keys, :], both))
+            if masked:
+                row = lax.broadcasted_iota(jnp.int32, (512, 256), 0)
+                column = lax.broadcasted_iota(jnp.int32, (512, 256), 1)
+                powers = jnp.where((row < 256) | (column >= 128), powers, 0.0)
+            prob = by_transpose(vz[keys, :], both) + ddrow[0:1, at]
+            score = (powers * prob).astype(bf)
+            dq_t[0:64, at] += product(k_t[:, keys], score)
+            return total + product(score, qz[at, :]) + product(powers.astype(bf), dz[at, :])
+
+        total = fold(jj, jnp.zeros((512, 128), f4), True)
+        if jj < 7:
+            total = lax.fori_loop(jj + 1, 8, fold, total)
+        part[keys, :] = total
+        exchange(jj)
+        if jj:
+            finish(jj - 1)
+    finish(7)
+    for k in range(1, CHIPS):
+        t = l.ahead(k)
+        l.send(rows_at(send_kv, t * 128, 128), rows_at(recv_kv, l.b * 128, 128), ks.at[k], kr.at[k], (l.h, t))
+        l.send(rows_at(send_q, t * 64, 64), rows_at(recv_q, l.b * 64, 64), qs.at[k], qr.at[k], (l.h, t))
+    recv_kv[pl.ds(pl.multiple_of(l.b * 128, 128), 128), :] = send_kv[pl.ds(pl.multiple_of(l.b * 128, 128), 128), :]
+    recv_q[pl.ds(pl.multiple_of(l.b * 64, 64), 64), :] = send_q[pl.ds(pl.multiple_of(l.b * 64, 64), 64), :]
+    for k in range(1, CHIPS):
+        l.arrived(rows_at(recv_kv, l.behind(k) * 128, 128), ks.at[k], kr.at[k])
+        l.arrived(rows_at(recv_q, l.behind(k) * 64, 64), qs.at[k], qr.at[k])
+    for p in range(8):
+        at = p * 128
+        one = recv_q[p * 128 : p * 128 + 64, :].astype(f4)
+        two = recv_q[p * 128 + 64 : p * 128 + 128, :].astype(f4)
+        joint_grad[0:64, at : at + 128] = jnp.where(low64, one, swap(two)).astype(bf)
+        joint_grad[64:128, at : at + 128] = jnp.where(low64, swap(one), two).astype(bf)
+        one = recv_kv[p * 256 : p * 256 + 128, :].astype(f4)
+        two = recv_kv[p * 256 + 128 : p * 256 + 256, :].astype(f4)
+        joint_grad[:, 1024 + at : 1152 + at] = jnp.where(low, one, swap(two)).astype(bf)
+        joint_grad[:, 2048 + at : 2176 + at] = jnp.where(low, swap(one), two).astype(bf)
+    l.settle()
+
+
+def back(kv, q, attden, agrad):
+    bf, f4 = jnp.bfloat16, jnp.float32
+    vmem = pl.BlockSpec(memory_space=pltpu.VMEM)
+    dma = pltpu.SemaphoreType.DMA
+    return pl.pallas_call(
+        back_kernel,
+        name="back",
+        in_specs=[vmem] * 4,
+        out_shape=jax.ShapeDtypeStruct((128, 3072), bf),
+        out_specs=vmem,
+        scratch_shapes=[
+            pltpu.VMEM((1024, 128), bf), pltpu.VMEM((1024, 128), bf),
+            pltpu.VMEM((2048, 128), bf), pltpu.VMEM((2048, 128), bf), pltpu.VMEM((2048, 128), bf),
+            pltpu.VMEM((4096, 128), bf), pltpu.VMEM((4096, 128), bf), pltpu.VMEM((64, 4096), bf),
+            pltpu.VMEM((1, 2048), f4), pltpu.VMEM((128, 2048), f4),
+            pltpu.VMEM((4096, 128), f4), pltpu.VMEM((2048, 128), f4),
+            pltpu.VMEM((2048, 128), bf), pltpu.VMEM((1024, 128), bf),
+            pltpu.VMEM((2048, 128), bf), pltpu.VMEM((1024, 128), bf),
+            dma((16,)), dma((16,)), dma((16,)), dma((16,)),
+            dma((16,)), dma((16,)), dma((16,)), dma((16,)),
+        ],
+        compiler_params=pltpu.CompilerParams(
+            collective_id=1, has_side_effects=True, vmem_limit_bytes=LIMIT
+        ),
+    )(kv, q, attden, agrad)
+
+
+def small_block(blocks, triple_bias, expand_bias):
+    place = lax.rem(shard_of(lax.axis_index("head"), lax.axis_index("blk")), 4)
+    lane = jnp.arange(128, dtype=jnp.int32)[None, :]
+    six = jnp.where(lane // 32 == place, jnp.tile(jnp.stack(blocks), (1, 4)), 0)
+    wide = jnp.arange(384, dtype=jnp.int32)
+    three = jnp.where(wide // 96 == place, jnp.tile(triple_bias, 4), 0).reshape(3, 128)
+    row = jnp.arange(4, dtype=jnp.int32)[:, None]
+    four = jnp.where(row == place, expand_bias[None, :], 0)
+    return jnp.concatenate([six, three, four, jnp.zeros((3, 128), jnp.bfloat16)], axis=0).astype(jnp.bfloat16)
+
+
+def local_fast(
+    hidden, adapter_index, first_gain, first_bias, triple_weight, triple_bias, mixer_weight, mixer_bias,
+    second_gain, second_bias, expand_weight, expand_bias, reduce_weight, reduce_bias, triple_down, triple_up,
+    mixer_down, mixer_up, expand_down, expand_up, reduce_down, reduce_up, cotangent,
+):
+    selection = selector(adapter_index)
+
+    def turned(factor):
+        return jnp.transpose(factor, (0, 2, 1)).reshape(ADAPTERS * RANK, factor.shape[1])
+
+    small_sh = small_block(
+        [first_gain, first_bias, mixer_bias, second_gain, second_bias, reduce_bias], triple_bias, expand_bias
+    )
+    down_t, up_t = turned(triple_down), flat_up(triple_up)
+    (wt, wm, wr, we, vecs, bias_e, first_normed, rank_triple, kv, q, attden, attended_low) = front(
+        hidden, selection, small_sh, triple_weight, mixer_weight, reduce_weight, expand_weight, down_t, up_t
+    )
+    stream = hidden.astype(jnp.float32)
+    gain_one, bias_one, bias_m, gain_two, bias_two, bias_r = [vecs[n] for n in range(6)]
+    down_m, up_m = turned(mixer_down), flat_up(mixer_up)
+    down_e, up_e = turned(expand_down), flat_up(expand_up)
+    down_r, up_r = turned(reduce_down), flat_up(reduce_up)
+
+    def first_norm(values_in):
+        return layer_norm(values_in, gain_one, bias_one)
+
+    def second_norm(values_in):
+        return layer_norm(values_in, gain_two, bias_two)
+
+    def forward(source, weight, offset, down, up):
+        low_rank = (selection * by_transpose(source, down)).astype(jnp.bfloat16)
+        return product(source, weight) + offset + product(low_rank, up), low_rank
+
+    def backward(source, low_rank, out_grad, down, up):
+        rank_grad = (selection * by_transpose(out_grad, up)).astype(jnp.bfloat16)
+        return transpose_by(rank_grad, source), transpose_by(low_rank, out_grad), product(rank_grad, down)
+
+    mixed, rank_mixer = forward(attended_low, wm, bias_m, down_m, up_m)
+    residual = stream + mixed
+    second_normed = second_norm(residual).astype(jnp.bfloat16)
+    expanded, rank_expand = forward(second_normed, we, bias_e[0], down_e, up_e)
+    activated = jax.nn.gelu(expanded, approximate=True).astype(jnp.bfloat16)
+    reduced, rank_reduce = forward(activated, wr, bias_r, down_r, up_r)
+    layer_out = (residual + reduced).astype(jnp.bfloat16)
+    reduce_down_grad, reduce_up_grad, through = backward(activated, rank_reduce, cotangent, down_r, up_r)
+    activated_grad = (by_transpose(cotangent, wr) + through).astype(jnp.bfloat16)
+    gelu_back = jax.vjp(lambda values_in: jax.nn.gelu(values_in, approximate=True), expanded)[1]
+    expanded_grad = gelu_back(activated_grad.astype(jnp.float32))[0].astype(jnp.bfloat16)
+    expand_down_grad, expand_up_grad, through = backward(second_normed, rank_expand, expanded_grad, down_e, up_e)
+    normed_grad = by_transpose(expanded_grad, we) + through
+    residual_grad = cotangent.astype(jnp.float32) + jax.vjp(second_norm, residual)[1](normed_grad)[0]
+    mixed_grad = residual_grad.astype(jnp.bfloat16)
+    mixer_down_grad, mixer_up_grad, through = backward(attended_low, rank_mixer, mixed_grad, down_m, up_m)
+    attended_grad = (by_transpose(mixed_grad, wm) + through).astype(jnp.bfloat16)
+    joint_tokens = back(kv, q, attden, attended_grad)
+    triple_down_grad, triple_up_grad, through = backward(first_normed, rank_triple, joint_tokens, down_t, up_t)
+    normed_one_grad = by_transpose(joint_tokens, wt) + through
+    hidden_grad = (residual_grad + jax.vjp(first_norm, stream)[1](normed_one_grad)[0]).astype(jnp.bfloat16)
+    summed = lax.psum(
+        (
+            triple_down_grad, triple_up_grad, mixer_down_grad, mixer_up_grad,
+            expand_down_grad, expand_up_grad, reduce_down_grad, reduce_up_grad,
+        ),
+        ("head", "blk"),
+    )
+
+    def down_out(gradient):
+        return jnp.transpose(gradient.reshape(ADAPTERS, RANK, gradient.shape[1]), (0, 2, 1))
+
+    return (
+        layer_out,
+        hidden_grad,
+        down_out(summed[0]),
+        unflat_up(summed[1]),
+        down_out(summed[2]),
+        unflat_up(summed[3]),
+        down_out(summed[4]),
+        unflat_up(summed[5]),
+        down_out(summed[6]),
+        unflat_up(summed[7]),
+    )
+
+
 def solution(mesh):
     placed = (
         P(("blk", "head"), None),
@@ -425,8 +1041,9 @@
         P(),
         P(("blk", "head"), None),
     )
+    fits = tuple(mesh.shape[name] for name in ("head", "blk")) == (2, CHIPS)
     return jax.shard_map(
-        local,
+        local_fast if fits else local,
         mesh=mesh,
         in_specs=placed,
         out_specs=(

time: 1070 us -> 614 us (0.57)
  Pallas kernels: 0 us -> 349 us
  waiting for transfers between devices: 416 us -> 177 us
  blocking collectives: 177 us -> 0 us
  matrix products: 181 us -> 43.8 us
  local copies, waits for them, and re-layouts: 145 us -> 15.5 us
  loops' own time: 79.8 us -> 0 us
  other arithmetic: 42 us -> 4.92 us
    pallas_call x0 -> x2, Pallas kernels: none -> 349 us  [the longest x1 296 us: front(): pl.pallas_call(front_kernel, name='front', in_specs=[vmem, vmem, hbm, hbm...]
    all_gather x8 -> x0, waiting for transfers between devices: 246 us -> none  [the longest x2 93.4 us: local(): lax.all_gather(payload[0], ('head', 'blk'), axis=0, tiled=True)]
    all_gather x2 -> x0, blocking collectives: 135 us -> none  [the longest x1 68.9 us: local(): lax.all_gather(payload[2], ('head', 'blk'), axis=0, tiled=True)]
    dot_general x32 -> x0, matrix products: 127 us -> none  [the longest x12 46.1 us: score_block(): jnp.einsum('qhd,khd->qhk', queries, keys_block, preferred_element_type=jn...]
    unnamed x189 -> x66, local copies, waits for them, and re-layouts: 105 us -> 12.8 us
    another operation x27 -> x0, loops' own time: 79.8 us -> none  [the longest x1 26.5 us: key_grad_fold(): return lax.scan(key_visiting, totals, shaped + (firsts,))[0]]
    unnamed x1 -> x0, blocking collectives: 41.6 us -> none
    add x26 -> x0, other arithmetic: 31.1 us -> none  [the longest x24 31.1 us: locate(): (shard_index % cycle_ways * head_ways + shard_index // cycle_ways) * toke...]
  transfers between devices with their start and end apart: 9 -> 1, of which waited for: 7 -> 1; matrix products, arithmetic and copies ran while one was open for 18% -> 2% of each run, Pallas kernels for 0% -> 0%
where the time goes in v1:
time: 614 us; the launch traced here: 605 us
  Pallas kernels  349 us (57%)
  waiting for transfers between devices  177 us (29%)
  matrix products  43.8 us (7%)
  local copies, waits for them, and re-layouts  15.5 us (3%)
  between operations  15 us (2%)
    pallas_call x1, Pallas kernels, front(): pl.pallas_call(front_kernel, name='front', in_specs=[vmem, vmem, hbm, hbm...  296 us
    psum x1, waiting for transfers between devices, local_fast(): lax.psum((triple_down_grad, triple_up_grad, mixer_down_grad, mixer_up_gra...  177 us
    pallas_call x1, Pallas kernels, back(): pl.pallas_call(back_kernel, name='back', in_specs=[vmem] * 4, out_shape=j...  53 us
    dot_general x11, matrix products, by_transpose(): lax.dot_general(left, right, (((1,), (1,)), ((), ())), preferred_element_...  19.8 us
    dot_general x10, matrix products, product(): return jnp.dot(left, right, preferred_element_type=jnp.float32)  13.7 us
    unnamed x66, local copies, waits for them, and re-layouts  12.8 us
  transfers between devices with their start and end apart: 1, of which 1 were waited for; matrix products, arithmetic and copies ran while one was open for 2% of the time, Pallas kernels for 0%

profile of v1, /device:TPU:1, one launch (start us, length us, event | category | flops | bytes accessed | tf_op | source)
XLA Modules:
  0.0 605.5 jit_solution(10081007224299127416)
XLA Ops:
  9.0 1.4 compare_convert_fusion.sel
  11.7 296.3 %front.1 = (bf16[1024,3072]{1,0:T(8,128)(2,1)}, bf16[1024,1024]{1,0:T(8,128)(2,1)}, bf16[4096,1024]{1,0:T(8,128)(2,1)}, bf16[1024,4096]{1,0:T(8,128)(2,1)}, f32[...) custom-call(bf16[128,1024]{1,0:T(8,128)(2,1)} %hidden.1, ...), custom_call_target="tpu_custom_call" | custom-call | tf_op jit(solution)/shard_map/front/pallas_call | solution.py:746
  309.0 1.2 fusion.18
  310.2 2.2 convolution_add_fusion.8
  313.0 6.4 %convolution_bitcast_fusion = f32[128,4096]{1,0:T(8,128)S(1)} fusion(bf16[4096,1024]{1,0:T(8,128)(2,1)} %get-tuple-element.27, bf16[128,1024]{1,0:T(8,128)(2,1)S(1)} %copy-done.5), kind=kOutput, calls=%fused_computation.1 | convolution fusion | flops 1073741824 | bytes 10747904 | tf_op jit(solution)/shard_map/dot_general | solution.py:27
  320.1 1.3 convolution_add_fusion.2
  322.6 1.7 fusion.8
  324.4 3.1 fusion.38
  330.7 1.0 fusion.44
  331.7 1.0 fusion.45
  332.8 1.8 fusion.46
  335.0 1.8 fusion.47
  338.8 53.0 %back.1 = bf16[128,3072]{1,0:T(8,128)(2,1)} custom-call(bf16[4096,128]{1,0:T(8,128)(2,1)} %get-tuple-element.28.kv, bf16[2048,128]{1,0:T(8,128)(2,1)} %get-tuple-element.29.q, f32[2048,128]{1,0:T(8,128)} %get-tuple-element.30.attden, bf16[128,1024]{1,0:T(8,128)(2,1)} %fusion.14.agrad), custom_call_target="tpu_custom_call" | custom-call | tf_op jit(solution)/shard_map/back/pallas_call | solution.py:901
  391.8 1.6 fusion.15
  393.4 1.5 fusion.42
  394.9 1.0 fusion.48
  396.0 1.0 fusion.41
  397.2 5.0 fusion.40
  402.9 4.7 convolution_add_fusion.9
  409.5 177.0 %all-reduce.3.cloned.1.call-done = (f32[8,1024,16]{1,2,0:T(8,128)}, f32[8,16,3072]{2,1,0:T(8,128)}, f32[8,1024,16]{1,2,0:T(8,128)}, f32[8,16,1024]{2,1,0:T(8,128...) async-done(((f32[8,1024,16]{1,2,0:T(8,128)}, f32[8,16,3072]{2,1,0:T(8,128)}, f32[8,1024,16]{1,2,0:T(8,128)}, ...) | async-done | bytes 8388624 | tf_op jit(solution)/shard_map/psum | solution.py:993
  586.5 1.9 copy.43
  588.5 2.8 copy.44
  593.7 1.3 copy.48
  596.0 1.3 copy.49
  (106 shorter events, 19.1 us)
Async XLA Ops:
  7.2 314.2 %copy-start = (bf16[8,16,4096]{2,1,0:T(8,128)(2,1)S(1)}, bf16[8,16,4096]{2,1,0:T(8,128)(2,1)}, u32[]{:S(2)}) copy-start(bf16[8,16,4096]{2,1,0:T(8,128)(2,1)} %param.42) | copy-start | bytes 3145732
  7.2 301.8 %copy-start.25 = (s32[128]{0:T(128)S(1)}, s32[128]{0:T(128)}, u32[]{:S(2)}) copy-start(s32[128]{0:T(128)} %param.24) | copy-start | bytes 1540
  7.2 301.8 %copy-start.18 = (bf16[8,1024,16]{1,2,0:T(8,128)(2,1)S(1)}, bf16[8,1024,16]{1,2,0:T(8,128)(2,1)}, u32[]{:S(2)}) copy-start(bf16[8,1024,16]{1,2,0:T(8,128)(2,1)} %param.39) | copy-start | bytes 786436
  7.2 579.3 %all-reduce.3.cloned.1.call-start = ((), (), s32[]{:S(2)}) async-start(), calls=%async_computation | async-start | bytes 16777216 | tf_op jit(solution)/shard_map/psum | solution.py:993
  308.0 4.4 copy-start.3
  308.0 4.4 copy-start.17
  310.2 2.7 copy-start.5
  312.9 7.1 %slice-start = ((s8[8388608]{0:T(1024)(128)(4,1)}), s8[4194304]{0:T(1024)(128)(4,1)S(1)}, s32[]{:S(2)}) async-start(s8[8388608]{0:T(1024)(128)(4,1)} %bitcast.106), calls=%async_computation.1 | async-start | bytes 8388608
  313.0 6.4 %copy-start.13 = (bf16[8,16,1024]{2,1,0:T(8,128)(2,1)S(1)}, bf16[8,16,1024]{2,1,0:T(8,128)(2,1)}, u32[]{:S(2)}) copy-start(bf16[8,16,1024]{2,1,0:T(8,128)(2,1)} %param.44) | copy-start | bytes 786436
  313.0 6.8 %copy-start.12 = (bf16[8,1024,16]{1,2,0:T(8,128)(2,1)S(1)}, bf16[8,1024,16]{1,2,0:T(8,128)(2,1)}, u32[]{:S(2)}) copy-start(bf16[8,1024,16]{1,2,0:T(8,128)(2,1)} %param.41) | copy-start | bytes 786436
  313.0 7.1 %slice-start.1 = ((s8[8388608]{0:T(1024)(128)(4,1)}), s8[4194304]{0:T(1024)(128)(4,1)S(1)}, s32[]{:S(2)}) async-start(s8[8388608]{0:T(1024)(128)(4,1)} %bitcast.106), calls=%async_computation.2 | async-start | bytes 8388608
  313.0 7.1 %copy-start.26 = (f32[1,4096]{1,0:T(1,128)S(1)}, f32[1,4096]{1,0:T(1,128)}, u32[]{:S(2)}) copy-start(f32[1,4096]{1,0:T(1,128)} %get-tuple-element.26) | copy-start | bytes 49156
  338.8 53.0 %copy-start.8 = (bf16[8,16,3072]{2,1,0:T(8,128)(2,1)S(1)}, bf16[8,16,3072]{2,1,0:T(8,128)(2,1)}, u32[]{:S(2)}) copy-start(bf16[8,16,3072]{2,1,0:T(8,128)(2,1)} %param.38) | copy-start | bytes 2359300
  338.8 54.6 %copy-start.24 = (bf16[128,128]{1,0:T(8,128)(2,1)S(1)}, bf16[128,128]{1,0:T(8,128)(2,1)}, u32[]{:S(2)}) copy-start(bf16[128,128]{1,0:T(8,128)(2,1)} %get-tuple-element.33) | copy-start | bytes 98308
  391.8 4.2 copy-start.23
  397.2 5.0 copy-start.15
  402.9 4.7 copy-start.14
  402.9 5.7 copy-start.7
  586.5 4.7 copy-start.22
  588.5 3.6 copy-start.21
  588.5 4.4 copy-start.20
  591.3 2.4 copy-start.11
  593.7 2.3 copy-start.10
  593.7 4.5 copy-start.1
  (6 other events, 9.7 us)
Sparse Core Ops, SparseCore 0:
  397.2 189.3 all-reduce.2

commit v2 on v0

--- a/solution.py
+++ b/solution.py
@@ -1,8 +1,12 @@
+import functools
 import math
+import types
 
 import jax
 import jax.numpy as jnp
 from jax import lax
+from jax.experimental import pallas as pl
+from jax.experimental.pallas import tpu as pltpu
 from jax.sharding import PartitionSpec as P
 
 WIDTH = 1024
@@ -399,6 +403,1107 @@
     )
 
 
+MESH = pl.DeviceIdType.MESH
+CHIPS = 16
+LIMIT = 62 * 1024 * 1024 - 512 * 1024
+BF = jnp.bfloat16
+F4 = jnp.float32
+
+
+ALONG = ((0, 1, 2, 3), (1, 0, 2, 3), (2, 1, 3, 0), (3, 2, 1, 0))
+
+
+class Links:
+    def __init__(self):
+        self.h = lax.axis_index("head")
+        self.b = lax.axis_index("blk")
+        self.o = 1 - self.h
+        self.sent = []
+        self.x = lax.rem(self.b, 2)
+        self.y = lax.rem(self.b // 2, 2)
+        self.z = self.b // 4
+        self.xb = self.b + 1 - 2 * self.x
+        self.yb = self.b + 2 - 4 * self.y
+        self.db = self.xb + 2 - 4 * self.y
+        self.columns = [lax.rem(chip, 4) for chip in (self.b, self.xb, self.yb, self.db)]
+
+    def nth(self, n):
+        return sum(jnp.where(self.z == z, table[n], 0) for z, table in enumerate(ALONG))
+
+    def at_line(self, z):
+        return lax.rem(self.b, 4) + 4 * z
+
+    def along(self, piece, sems, index):
+        for k, wanted in ((1, self.z < 3), (3, self.z > 0), (2, None)):
+            where = (piece, piece, sems, index + (self.z,), (self.h, self.ahead(4 * k)))
+            if wanted is None:
+                self.send(*where)
+            else:
+                self.send_if(wanted, *where)
+
+    def pass_on(self, piece, z, sems, index):
+        wanted = (self.z == 2) & (z == 0) | (self.z == 1) & (z == 3)
+        chip = self.columns[0] + 4 * (3 - z)
+        self.send_if(wanted, piece, piece, sems, index + (z,), (self.h, chip))
+
+    def ahead(self, k):
+        return lax.rem(self.b + k, CHIPS)
+
+    def behind(self, k):
+        return lax.rem(self.b + CHIPS - k, CHIPS)
+
+    def greet(self):
+        barrier = pltpu.get_barrier_semaphore()
+        for k in range(1, CHIPS):
+            pl.semaphore_signal(
+                barrier, 1, device_id=(self.h, self.ahead(k)), device_id_type=MESH
+            )
+        pl.semaphore_signal(barrier, 1, device_id=(self.o, self.b), device_id_type=MESH)
+
+    def met(self):
+        pl.semaphore_wait(pltpu.get_barrier_semaphore(), CHIPS)
+
+    def copy(self, source, target, sems, at, device):
+        return pltpu.make_async_remote_copy(
+            src_ref=source,
+            dst_ref=target,
+            send_sem=sems[0].at[at],
+            recv_sem=sems[1].at[at],
+            device_id=device,
+            device_id_type=MESH,
+        )
+
+    def send(self, source, target, sems, at, device):
+        copy = self.copy(source, target, sems, at, device)
+        copy.start()
+        self.sent.append((None, copy))
+
+    def send_if(self, wanted, *where):
+        copy = self.copy(*where)
+        pl.when(wanted)(copy.start)
+        self.sent.append((wanted, copy))
+
+    def arrived(self, target, sems, at):
+        self.copy(target, target, sems, at, (self.o, self.b)).wait_recv()
+
+    def settle(self):
+        for wanted, copy in self.sent:
+            if wanted is None:
+                copy.wait_send()
+            else:
+                pl.when(wanted)(copy.wait_send)
+        self.sent = []
+
+
+class Exchange:
+    def __init__(self, links, source, target, rows, sems, slot=None):
+        self.links, self.source, self.target = links, source, target
+        self.rows, self.sems = rows, sems
+        self.slot = slot or (lambda chip: rows_at(target, chip * rows, rows))
+
+    def send(self, t):
+        l = self.links
+
+        @pl.when(l.b != t)
+        def _():
+            l.copy(
+                rows_at(self.source, t * self.rows, self.rows),
+                self.slot(l.b), self.sems, lax.rem(t + CHIPS - l.b, CHIPS), (l.h, t),
+            ).start()
+
+    def own(self):
+        l = self.links
+        copy = pltpu.make_async_copy(
+            rows_at(self.source, l.b * self.rows, self.rows), self.slot(l.b), self.sems[0].at[0]
+        )
+        copy.start()
+        copy.wait()
+
+    def wait(self, k):
+        self.links.arrived(self.slot(self.links.behind(k)), self.sems, k)
+
+    def settle(self):
+        for k in range(1, CHIPS):
+            l = self.links
+            part = rows_at(self.source, l.ahead(k) * self.rows, self.rows)
+            l.copy(part, part, self.sems, k, (l.h, l.ahead(k))).wait_send()
+
+
+def half_mask(rows):
+    return lax.broadcasted_iota(jnp.int32, (rows, 128), 1) < 64
+
+
+def swap(tile):
+    return pltpu.roll(tile, 64, 1)
+
+
+def rows_at(ref, start, count):
+    return ref.at[pl.ds(pl.multiple_of(start, 16), count), :]
+
+
+class Gather:
+    def __init__(self, links, number, slot, sems):
+        self.links, self.p, self.slot = links, number, slot
+        self.sems = sems
+
+    def send(self, axis, n, chip, device):
+        piece = self.slot(self.links.h, chip)
+        self.links.send(piece, piece, self.sems[axis], (self.p, n), device)
+
+    def chip(self, side, n):
+        return side + 4 * self.links.nth(n)
+
+    def own(self, n):
+        l = self.links
+        chip = self.chip(l.columns[0], n)
+        if n:
+            l.pass_on(self.slot(l.h, chip), l.nth(n), self.sems["z"], (self.p,))
+        else:
+            l.along(self.slot(l.h, chip), self.sems["z"], (self.p,))
+        self.send("x", n, chip, (l.h, l.xb))
+        self.send("y", n, chip, (l.h, l.yb))
+        self.send("c", n, chip, (l.o, l.b))
+
+    def from_line(self, n):
+        l = self.links
+        chip = self.chip(l.columns[0], n)
+        l.arrived(self.slot(l.h, chip), self.sems["z"], (self.p, l.nth(n)))
+        self.own(n)
+
+    def arrived(self, axis, n, chip):
+        self.links.arrived(self.slot(self.links.h, chip), self.sems[axis], (self.p, n))
+
+    def from_side(self, axis, n):
+        l = self.links
+        chip = self.chip(l.columns[1 if axis == "x" else 2], n)
+        self.arrived(axis, n, chip)
+        if (n % 2 == 0) == (axis == "x"):
+            self.send("d", n, chip, (l.h, l.yb if axis == "x" else l.xb))
+        self.send("c", (4 if axis == "x" else 8) + n, chip, (l.o, l.b))
+
+    def from_corner(self, n):
+        l = self.links
+        chip = self.chip(l.columns[3], n)
+        self.arrived("d", n, chip)
+        self.send("c", 12 + n, chip, (l.o, l.b))
+
+    def stages(self):
+        part = functools.partial
+        return [
+            [part(self.own, 0)],
+            [part(self.from_line, 1), part(self.from_side, "x", 0), part(self.from_side, "y", 0), part(self.from_line, 2)],
+            [part(self.from_side, axis, 1) for axis in "xy"]
+            + [part(self.from_line, 3)]
+            + [part(self.from_side, axis, n) for n in (2, 3) for axis in "xy"],
+            [part(self.from_corner, n) for n in range(4)],
+        ]
+
+    def whole(self):
+        l = self.links
+        for number in range(16):
+            chip = self.chip(l.columns[number // 4], number % 4)
+            l.arrived(self.slot(l.o, chip), self.sems["c"], (self.p, number))
+
+
+class RowSlice:
+    def __init__(self, links, ref, sems):
+        self.links, self.ref = links, ref
+        self.line_sems, self.core_sems = sems
+
+    def slot(self, h, z):
+        return rows_at(self.ref, (h * 4 + z) * 128, 128)
+
+    def core(self, k, z):
+        l = self.links
+        l.send(self.slot(l.h, z), self.slot(l.h, z), self.core_sems, k, (l.o, l.b))
+
+    def own(self, n):
+        l = self.links
+        z = l.nth(n)
+        if n:
+            l.pass_on(self.slot(l.h, z), z, self.line_sems, ())
+        else:
+            l.along(self.slot(l.h, z), self.line_sems, ())
+        self.core(n, z)
+
+    def from_line(self, n):
+        l = self.links
+        z = l.nth(n)
+        l.arrived(self.slot(l.h, z), self.line_sems, (z,))
+        self.own(n)
+
+    def stages(self):
+        part = functools.partial
+        return [[part(self.own, 0)], [part(self.from_line, 1)], [part(self.from_line, 2)], [part(self.from_line, 3)]]
+
+    def whole(self):
+        l = self.links
+        for n in range(4):
+            l.arrived(self.slot(l.o, l.nth(n)), self.core_sems, n)
+
+
+class ColumnSlice:
+    def __init__(self, links, ref, stage, sems):
+        self.links, self.ref, self.stage = links, ref, stage
+        self.plane_sems, self.line_sems, self.core_sems = sems
+
+    def chip(self, j, n):
+        return self.links.columns[j] + 4 * self.links.nth(n)
+
+    def slot(self, h, chip):
+        return rows_at(self.ref, shard_of(h, chip) * 32, 32)
+
+    def own(self, j, n):
+        l = self.links
+        piece = self.slot(l.h, self.chip(j, n))
+        if n:
+            l.pass_on(piece, l.nth(n), self.line_sems, (j,))
+        else:
+            l.along(piece, self.line_sems, (j,))
+        l.send(piece, piece, self.core_sems, (j, n), (l.o, l.b))
+
+    def start(self):
+        l = self.links
+        for j, chip in enumerate((l.b, l.xb, l.yb, l.db)):
+            if j:
+                l.send(rows_at(self.stage, j * 32, 32), self.slot(l.h, l.b), self.plane_sems, j, (l.h, chip))
+
+    def from_plane(self, j):
+        self.links.arrived(self.slot(self.links.h, self.chip(j, 0)), self.plane_sems, j)
+        self.own(j, 0)
+
+    def from_line(self, j, n):
+        l = self.links
+        l.arrived(self.slot(l.h, self.chip(j, n)), self.line_sems, (j, l.nth(n)))
+        self.own(j, n)
+
+    def stages(self):
+        part = functools.partial
+        return [
+            [self.start],
+            [part(self.own, 0, 0)] + [part(self.from_plane, j) for j in range(1, 4)],
+            [part(self.from_line, j, n) for n in range(1, 4) for j in range(4)],
+        ]
+
+    def whole(self):
+        l = self.links
+        for j in range(4):
+            for n in range(4):
+                l.arrived(self.slot(l.o, self.chip(j, n)), self.core_sems, (j, n))
+
+
+def ordered(stages, lag):
+    events = []
+    deepest = max(len(stage) for stage in stages)
+    for tick in range(len(stages) * lag + deepest):
+        for n, stage in enumerate(stages):
+            if 0 <= tick - n * lag < len(stage):
+                events += stage[tick - n * lag]
+    return events
+
+
+class Reduce:
+    def __init__(self, links, g, out, base, width, bufs, sems):
+        self.l, self.g, self.out, self.base, self.sems = links, g, out, base, sems
+        self.by_core, self.by_side, self.by_turn, self.by_line = bufs
+        self.half, self.p = width // 2, width // 4
+        l = links
+        self.mine = base + l.h * self.half
+        p = self.p
+        self.keep1 = (self.mine + l.x * (p // 2), self.mine + p + l.y * (p // 2))
+        self.give1 = (self.mine + (1 - l.x) * (p // 2), self.mine + p + (1 - l.y) * (p // 2))
+        self.keep2 = (self.keep1[0] + l.y * (p // 4), self.keep1[1] + l.x * (p // 4))
+        self.give2 = (self.keep1[0] + (1 - l.y) * (p // 4), self.keep1[1] + (1 - l.x) * (p // 4))
+
+    def at(self, start, width):
+        return self.g.at[:, pl.ds(pl.multiple_of(start, 128), width)]
+
+    def out_at(self, start, width):
+        return self.out.at[:, pl.ds(pl.multiple_of(start, 128), width)]
+
+    def chunk(self, z):
+        first, second = self.keep2
+        return first * (1 - z // 2) + second * (z // 2) + lax.rem(z, 2) * (self.p // 8)
+
+    def add(self, start, width, others, final=False):
+        tile = 384 if width % 384 == 0 else 128
+        for n in range(width // tile):
+            here = pl.ds(pl.multiple_of(start + n * tile, 128), tile)
+            total = self.g[:, here].astype(F4)
+            for other in others:
+                total = total + other[:, n * tile : (n + 1) * tile].astype(F4)
+            (self.out if final else self.g)[:, here] = total.astype(BF)
+
+    def steps(self):
+        l, p = self.l, self.p
+        sides, turns = (l.xb, l.yb), (l.yb, l.xb)
+
+        def cores():
+            away = self.base + l.o * self.half
+            l.send(self.at(away, self.half), self.by_core, self.sems, 0, (l.o, l.b))
+
+        def side():
+            l.arrived(self.by_core, self.sems, 0)
+            for n in range(2):
+                self.add(self.give1[n], p // 2, [self.by_core.at[:, pl.ds(pl.multiple_of(self.give1[n] - self.mine, 128), p // 2)]])
+                l.send(self.at(self.give1[n], p // 2), self.by_side.at[n], self.sems, 1 + n, (l.h, sides[n]))
+            for n in range(2):
+                self.add(self.keep1[n], p // 2, [self.by_core.at[:, pl.ds(pl.multiple_of(self.keep1[n] - self.mine, 128), p // 2)]])
+
+        def turn():
+            for n in range(2):
+                l.arrived(self.by_side.at[n], self.sems, 1 + n)
+                self.add(self.keep1[n], p // 2, [self.by_side.at[n]])
+                l.send(self.at(self.give2[n], p // 4), self.by_turn.at[n], self.sems, 3 + n, (l.h, turns[n]))
+
+        def line():
+            for n in range(2):
+                l.arrived(self.by_turn.at[n], self.sems, 3 + n)
+                self.add(self.keep2[n], p // 4, [self.by_turn.at[n]])
+            for k in range(1, 4):
+                away = self.chunk(lax.rem(l.z + k, 4))
+                l.send(self.at(away, p // 8), self.by_line.at[k - 1], self.sems, 4 + k, (l.h, l.ahead(4 * k)))
+
+        def line_back():
+            for k in range(1, 4):
+                l.arrived(self.by_line.at[k - 1], self.sems, 4 + k)
+            self.add(self.chunk(l.z), p // 8, [self.by_line.at[k] for k in range(3)], True)
+            here = self.out_at(self.chunk(l.z), p // 8)
+            for k in range(1, 4):
+                l.send(here, here, self.sems, 7 + k, (l.h, l.ahead(4 * k)))
+
+        def turn_back():
+            for k in range(1, 4):
+                l.arrived(self.out_at(self.chunk(lax.rem(l.z + 4 - k, 4)), p // 8), self.sems, 7 + k)
+            for n in range(2):
+                here = self.out_at(self.keep2[n], p // 4)
+                l.send(here, here, self.sems, 11 + n, (l.h, turns[n]))
+
+        def side_back():
+            for n in range(2):
+                l.arrived(self.out_at(self.give2[n], p // 4), self.sems, 11 + n)
+                here = self.out_at(self.keep1[n], p // 2)
+                l.send(here, here, self.sems, 13 + n, (l.h, sides[n]))
+
+        def cores_back():
+            for n in range(2):
+                l.arrived(self.out_at(self.give1[n], p // 2), self.sems, 13 + n)
+            here = self.out_at(self.mine, self.half)
+            l.send(here, here, self.sems, 15, (l.o, l.b))
+
+        def done():
+            l.arrived(self.out_at(self.base + l.o * self.half, self.half), self.sems, 15)
+
+        return [cores, side, turn, line, line_back, turn_back, side_back, cores_back, done]
+
+
+class SliceReduce:
+    def __init__(self, links, g, out, base, bufs, sems):
+        self.l, self.g, self.out, self.base, self.sems = links, g, out, base, sems
+        self.by_core, self.by_line = bufs
+
+    def at(self, ref, start, width):
+        return ref.at[:, pl.ds(pl.multiple_of(start, 128), width)]
+
+    def steps(self):
+        l = self.l
+        chips = (l.b, l.xb, l.yb, l.db)
+        places = [
+            self.base + 2048 * (lax.rem(chip, 4)) for chip in chips
+        ]
+
+        def region(j, h, z=None):
+            if z is None:
+                return self.at(self.out, places[j] + h * 1024, 1024)
+            return self.at(self.out, places[j] + h * 1024 + z * 256, 256)
+
+        def cores():
+            l.send(self.at(self.g, l.o * 1024, 1024), self.by_core, self.sems, 0, (l.o, l.b))
+
+        def line():
+            l.arrived(self.by_core, self.sems, 0)
+            for n in range(4):
+                here = pl.ds(pl.multiple_of(l.h * 1024 + n * 256, 128), 256)
+                total = self.g[:, here].astype(F4) + self.by_core[:, n * 256 : (n + 1) * 256].astype(F4)
+                self.g[:, here] = total.astype(BF)
+            for k in range(1, 4):
+                z = lax.rem(l.z + k, 4)
+                l.send(self.at(self.g, l.h * 1024 + z * 256, 256), self.by_line.at[k - 1], self.sems, k, (l.h, l.ahead(4 * k)))
+
+        def line_back():
+            total = self.g[:, pl.ds(pl.multiple_of(l.h * 1024 + l.z * 256, 128), 256)].astype(F4)
+            for k in range(1, 4):
+                l.arrived(self.by_line.at[k - 1], self.sems, k)
+                total = total + self.by_line[k - 1].astype(F4)
+            self.out[:, pl.ds(pl.multiple_of(places[0] + l.h * 1024 + l.z * 256, 128), 256)] = total.astype(BF)
+            for k in range(1, 4):
+                l.send(region(0, l.h, l.z), region(0, l.h, l.z), self.sems, 3 + k, (l.h, l.ahead(4 * k)))
+
+        def plane():
+            for k in range(1, 4):
+                l.arrived(region(0, l.h, lax.rem(l.z + 4 - k, 4)), self.sems, 3 + k)
+            for j in range(1, 4):
+                l.send(region(0, l.h), region(0, l.h), self.sems, 6 + j, (l.h, chips[j]))
+            l.send(region(0, l.h), region(0, l.h), self.sems, 10, (l.o, l.b))
+
+        def cores_back():
+            for j in range(1, 4):
+                l.arrived(region(j, l.h), self.sems, 6 + j)
+                l.send(region(j, l.h), region(j, l.h), self.sems, 10 + j, (l.o, l.b))
+
+        def done():
+            for j in range(4):
+                l.arrived(region(j, l.o), self.sems, 10 + j)
+
+        return [cores, line, line_back, plane, cores_back, done]
+
+
+def shard_of(h, chip):
+    return h * CHIPS + chip
+
+
+def centre(stream):
+    average = jnp.mean(stream, axis=-1, keepdims=True)
+    centred = stream - average
+    variance = jnp.mean(centred * centred, axis=-1, keepdims=True)
+    scale = lax.rsqrt(variance + EPSILON)
+    return centred * scale, scale
+
+
+def norm_back(stream, gain, grad):
+    hat, scale = centre(stream)
+    q = grad * gain
+    return scale * (
+        q - jnp.mean(q, axis=-1, keepdims=True) - hat * jnp.mean(q * hat, axis=-1, keepdims=True)
+    )
+
+
+def gelu_parts(u):
+    cubic = 0.044715 * u * u
+    slope = math.sqrt(2.0 / math.pi)
+    t = jnp.tanh(slope * u * (1.0 + cubic))
+    grown = 0.5 * (1.0 + t)
+    return u * grown, grown + 0.5 * u * (1.0 - t * t) * slope * (1.0 + 3.0 * cubic)
+
+
+PIECES = 5
+MIXER_D, MIXER_U, EXPAND_D, REDUCE_U, TRIPLE_D, TRIPLE_U, SLICES, COLUMNS = (
+    0, 1024, 2048, 3072, 4096, 5120, 8192, 16384,
+)
+
+INPUTS = (
+    "hidden", "cot", "sel", "small_sh", "triple_sh", "mixer_sh", "reduce_sh", "expand_sh",
+    "down_t", "up_t", "down_m", "up_m", "down_e", "up_e", "down_r", "up_r",
+)
+OUTPUTS = {"layer_out": ((128, 1024), BF), "hidden_grad": ((128, 1024), BF), "g": ((128, COLUMNS), BF)}
+SCRATCH = {
+    "wt": ((1024, 3072), BF), "wm": ((1024, 1024), BF), "wr": ((1024, 1024), BF), "we": ((1024, 1024), BF),
+    "e_in": ((32, 4096), BF), "e_stage": ((128, 1024), BF), "up_es": ((128, 1024), BF), "down_rs": ((128, 1024), BF), "bias_es": ((1, 1024), F4),
+    "small": ((512, 128), BF), "vecs": ((16, 1024), F4), "bias_t": ((1, 3072), F4), "bias_e": ((1, 4096), F4),
+    "fn": ((128, 1024), BF), "rank_t": ((128, 128), BF), "kv": ((4096, 128), BF), "q": ((2048, 128), BF),
+    "attden": ((2048, 128), F4), "attended": ((128, 1024), BF), "ones_v": ((4096, 128), BF),
+    "send_kv": ((2048, 128), BF), "send_q": ((1024, 128), BF), "recv_q": ((1024, 128), BF),
+    "send_a": ((1024, 128), BF), "recv_a": ((1024, 128), BF),
+    "residual": ((128, 1024), F4), "sn_all": ((512, 1152), BF), "cot_all": ((512, 1152), BF),
+    "act": ((512, 1024), BF), "agrad": ((512, 1024), BF), "ng_part": ((512, 1152), BF), "ng_recv": ((512, 1152), BF),
+    "red_part": ((512, 1152), BF), "red_recv": ((512, 1152), BF),
+    "send_g": ((1024, 128), BF), "recv_g": ((1024, 128), BF),
+    "qd": ((2048, 128), BF), "dz": ((2048, 128), BF), "vz": ((4096, 128), BF),
+    "k_t": ((64, 4096), BF), "ddrow": ((1, 2048), F4), "dq_t": ((128, 2048), F4), "part": ((4096, 128), F4),
+    "recv_part": ((2048, 128), F4), "send_dkv": ((2048, 128), BF), "send_dq": ((1024, 128), BF),
+    "recv_dkv": ((2048, 128), BF), "recv_dq": ((1024, 128), BF), "jg": ((128, 3072), BF),
+"gp": ((128, SLICES), BF), "gs": ((128, 2048), BF), "slice_c": ((128, 1024), BF), "slice_l": ((3, 128, 256), BF),
+    "early_c": ((128, 2048), BF), "early_1": ((2, 128, 512), BF), "early_2": ((2, 128, 256), BF), "early_3": ((3, 128, 128), BF),
+    "late_c": ((128, 2048), BF), "late_1": ((2, 128, 512), BF), "late_2": ((2, 128, 256), BF), "late_3": ((3, 128, 128), BF),
+}
+SEMS = {
+    "z": (PIECES, 4), "x": (PIECES, 4), "y": (PIECES, 4), "d": (PIECES, 4), "c": (PIECES, 16),
+    "kv": (16,), "q": (16,), "f": (16,), "a": (16,), "g": (16,), "e": (16,), "dkv": (16,), "dq": (16,),
+    "early": (16,), "late": (16,), "slice": (16,),
+    "rz": (4,), "rc": (4,), "ep": (4,), "ez": (4, 4), "ec": (4, 4), "ct": (2, 4), "sn": (2, 4), "ng": (2, 4), "rd": (2, 4),
+}
+
+
+def layer_kernel(*refs):
+    names = list(INPUTS) + list(OUTPUTS) + list(SCRATCH)
+    r = types.SimpleNamespace(**dict(zip(names, refs)))
+    rest = refs[len(names) :]
+    local_sem = rest[0]
+    sems = {name: (rest[1 + 2 * n], rest[2 + 2 * n]) for n, name in enumerate(SEMS)}
+    l = Links()
+    low, low64 = half_mask(128), half_mask(64)
+    mine = shard_of(l.h, l.b)
+    local_copies = [
+        pltpu.make_async_copy(r.small_sh, rows_at(r.small, mine * 16, 16), local_sem.at[0]),
+        pltpu.make_async_copy(r.triple_sh, rows_at(r.wt, mine * 32, 32), local_sem.at[1]),
+        pltpu.make_async_copy(r.mixer_sh, rows_at(r.wm, mine * 32, 32), local_sem.at[2]),
+        pltpu.make_async_copy(r.reduce_sh, rows_at(r.wr, (l.h * 4 + l.z) * 128, 128), local_sem.at[3]),
+        pltpu.make_async_copy(r.expand_sh, r.e_in, local_sem.at[4]),
+    ]
+    for copy in local_copies:
+        copy.start()
+    l.greet()
+
+    def columns(ref, at):
+        return lambda h, chip: ref.at[
+            pl.ds(pl.multiple_of(shard_of(h, chip) * 32, 32), 32), at : at + 1024
+        ]
+
+    slots = [lambda h, chip: rows_at(r.small, shard_of(h, chip) * 16, 16)]
+    slots += [columns(r.wt, m * 1024) for m in range(3)]
+    slots += [columns(r.wm, 0)]
+    pieces = [Gather(l, n, slot, sems) for n, slot in enumerate(slots)]
+    pieces.append(RowSlice(l, r.wr, (sems["rz"], sems["rc"])))
+    pieces.append(ColumnSlice(l, r.we, r.e_stage, (sems["ep"], sems["ez"], sems["ec"])))
+    places = [lax.rem(chip, 4) for chip in (l.b, l.xb, l.yb, l.db)]
+
+    def block(j, i):
+        return pl.ds(pl.multiple_of((i // 4 * 16 + places[j] + i % 4 * 4) * 128, 128), 128)
+
+    for i in range(8):
+        here = slice(i * 128, (i + 1) * 128)
+        r.up_es[:, here] = r.up_e[:, block(0, i)]
+        r.down_rs[:, here] = r.down_r[:, block(0, i)]
+    for copy in local_copies:
+        copy.wait()
+    for i in range(8):
+        here = slice(i * 128, (i + 1) * 128)
+        r.we[pl.ds(pl.multiple_of(mine * 32, 32), 32), here] = r.e_in[:, block(0, i)]
+        for j in range(1, 4):
+            r.e_stage[j * 32 : (j + 1) * 32, here] = r.e_in[:, block(j, i)]
+    l.met()
+    stages = [piece.stages() for piece in pieces]
+    events = [event for n in (0, 1, 2, 3, 6) for event in stages[n].pop(0)]
+    stages[2][1] += stages[5].pop(0)
+    events += ordered(stages[:4], 1)
+    ends = {n: len(events) for n in range(4)}
+    begun = len(events) + 1
+    events += stages[4].pop(0)
+    crossed = len(events) + 8
+    events += [event for stage in stages[4] for event in stage]
+    ends[4] = len(events)
+    events += stages[6].pop(0)
+    kicked = len(events)
+    events += [event for stage in stages[5] for event in stage]
+    ends[5] = len(events)
+    events += [event for stage in stages[6] for event in stage]
+    ends[6] = len(events)
+    state = [0]
+
+    def pump(count):
+        until(state[0] + count)
+
+    def until(end):
+        end = min(end, len(events))
+        while state[0] < end:
+            events[state[0]]()
+            state[0] += 1
+
+    def need(first, last):
+        until(ends[last])
+        for n in range(first, last + 1):
+            pieces[n].whole()
+
+    until(ends[3] - 4)
+    pieces[0].whole()
+    for g in range(8):
+        tile = jnp.zeros((16, 128), F4)
+        for n in range(4):
+            at = (4 * g + n) * 16
+            tile = tile + r.small[at : at + 16, :].astype(F4)
+        r.vecs[:, g * 128 : (g + 1) * 128] = tile
+        for n in range(3):
+            at = (g * 3 + n) * 128
+            r.bias_t[0:1, at : at + 128] = tile[6 + n : 7 + n, :]
+        for n in range(4):
+            at = (g * 4 + n) * 128
+            r.bias_e[0:1, at : at + 128] = tile[9 + n : 10 + n, :]
+    gain_one, bias_one, bias_m, gain_two, bias_two, bias_r = [
+        (lambda n=n: r.vecs[n : n + 1, :]) for n in range(6)
+    ]
+    hat, _ = centre(r.hidden[...].astype(F4))
+    r.fn[...] = (hat * gain_one() + bias_one()).astype(BF)
+
+    def rank(source, down):
+        return (r.sel[...] * by_transpose(source, down)).astype(BF)
+
+    r.rank_t[...] = rank(r.fn[...], r.down_t[...])
+    need(1, 3)
+    until(begun)
+
+    own = l.b * 256 + l.h * 128
+
+    def kv_at(chip, h):
+        return rows_at(r.kv, chip * 256 + h * 128, 128)
+
+    kv_out = Exchange(l, r.send_kv, r.kv, 128, sems["kv"], lambda chip: kv_at(chip, l.h))
+    q_out = Exchange(l, r.send_q, r.recv_q, 64, sems["q"])
+    for step in range(4):
+        plane = lax.rem(l.z + 1 + step, 4)
+
+        def joint(part):
+            at = pl.ds(pl.multiple_of(part * 1024 + plane * 256, 256), 256)
+            tile = (
+                product(r.fn[...], r.wt[:, at]) + r.bias_t[0:1, at] + product(r.rank_t[...], r.up_t[:, at])
+            )
+            return tile[:, :128], tile[:, 128:]
+
+        for n, (qt, kt, vt) in enumerate(zip(joint(0), joint(1), joint(2))):
+            c = plane * 4 + n * 2
+            send_kv, send_q = rows_at(r.send_kv, c * 128, 256), rows_at(r.send_q, c * 64, 128)
+            send_kv[0:128, :] = jnp.where(low, kt, swap(vt)).astype(BF)
+            send_kv[128:256, :] = jnp.where(low, swap(kt), vt).astype(BF)
+            qt = qt.astype(BF).astype(F4) * 0.125
+            turned = swap(qt)
+            send_q[0:64, :] = jnp.where(low64, qt[:64], turned[64:]).astype(BF)
+            send_q[64:128, :] = jnp.where(low64, turned[:64], qt[64:]).astype(BF)
+        for n in range(4):
+            kv_out.send(plane * 4 + n)
+            q_out.send(plane * 4 + n)
+    kv_out.own()
+    q_out.own()
+    until(crossed)
+    rank_grad_r = rank(r.cot[...], r.up_r[...])
+    for i in range(8):
+        r.bias_es[0:1, i * 128 : (i + 1) * 128] = r.bias_e[0:1, block(0, i)]
+
+    def to_plane(source, target, name, half, own):
+        for j, chip in ((3, l.db), (1, l.xb), (2, l.yb)):
+            part = rows_at(source, half * 256 + (0 if own else j * 64), 64)
+            l.send(part, rows_at(target, half * 256 + j * 64, 64), sems[name], (half, j), (l.h, chip))
+
+    def from_plane(target, name, half):
+        for j in range(1, 4):
+            l.arrived(rows_at(target, half * 256 + j * 64, 64), sems[name], (half, j))
+
+    def keep_own(target, at, tile):
+        target[0:64, at] = tile[:64]
+        target[256:320, at] = tile[64:]
+
+    all_columns, ranks = slice(0, 1024), slice(1024, 1152)
+    keep_own(r.cot_all, all_columns, r.cot[...])
+    keep_own(r.cot_all, ranks, rank_grad_r)
+    l.send(kv_at(l.b, l.h), kv_at(l.b, l.h), sems["f"], 0, (l.o, l.b))
+    for k in range(1, CHIPS):
+        kv_out.wait(k)
+        c = l.behind(k)
+        l.send(kv_at(c, l.h), kv_at(c, l.h), sems["f"], k, (l.o, l.b))
+        until(min(state[0] + 1, ends[4]))
+    until(kicked)
+    to_plane(r.cot_all, r.cot_all, "ct", 0, True)
+    to_plane(r.cot_all, r.cot_all, "ct", 1, True)
+    until(ends[5])
+    for k in range(1, CHIPS):
+        q_out.wait(k)
+    for k in range(CHIPS):
+        l.arrived(kv_at(l.behind(k), l.o), sems["f"], k)
+
+    for n in range(CHIPS):
+        tile = r.recv_q[n * 64 : n * 64 + 64, :].astype(F4)
+        r.q[n * 128 : n * 128 + 64, :] = jnp.where(low64, tile, 0.0).astype(BF)
+        r.q[n * 128 + 64 : n * 128 + 128, :] = jnp.where(low64, swap(tile), 0.0).astype(BF)
+        tile = r.kv[n * 256 : n * 256 + 256, :].astype(F4)
+        r.ones_v[n * 256 : n * 256 + 256, :] = jnp.where(half_mask(256), 1.0, tile).astype(BF)
+    a_out = Exchange(l, r.send_a, r.recv_a, 64, sems["a"])
+    for i in range(8):
+        queries = r.q[i * 256 : (i + 1) * 256, :]
+
+        def fold(jj, total, masked=False):
+            at = pl.ds(pl.multiple_of(jj * 512, 512), 512)
+            powers = jnp.exp(by_transpose(queries, r.kv[at, :]))
+            if masked:
+                row = lax.broadcasted_iota(jnp.int32, (256, 512), 0)
+                column = lax.broadcasted_iota(jnp.int32, (256, 512), 1)
+                powers = jnp.where((row >= 128) | (column < 256), powers, 0.0)
+            return total + product(powers.astype(BF), r.ones_v[at, :])
+
+        total = fold(i, jnp.zeros((256, 128), F4), True)
+        if i:
+            total = lax.fori_loop(0, i, fold, total)
+        share = total / swap(total)
+        r.attden[i * 256 : (i + 1) * 256, :] = jnp.where(half_mask(256), total, share)
+        for n in range(2):
+            t = 2 * i + n
+            part = share[n * 128 : n * 128 + 128]
+            packed = jnp.where(low64, swap(part[64:]), part[:64]).astype(BF)
+            r.send_a[t * 64 : t * 64 + 64, :] = packed
+            a_out.send(t)
+    a_out.own()
+    until(ends[6])
+    need(4, 4)
+    for k in range(1, CHIPS):
+        a_out.wait(k)
+    for p in range(8):
+        one = r.recv_a[p * 128 : p * 128 + 64, :].astype(F4)
+        two = r.recv_a[p * 128 + 64 : p * 128 + 128, :].astype(F4)
+        at = p * 128
+        r.attended[0:64, at : at + 128] = jnp.where(low64, swap(one), two).astype(BF)
+        r.attended[64:128, at : at + 128] = jnp.where(low64, one, swap(two)).astype(BF)
+
+    rank_m = rank(r.attended[...], r.down_m[...])
+    r.residual[...] = (
+        r.hidden[...].astype(F4)
+        + product(r.attended[...], r.wm[...])
+        + bias_m()
+        + product(rank_m, r.up_m[...])
+    )
+    hat, _ = centre(r.residual[...])
+    second_normed = (hat * gain_two() + bias_two()).astype(BF)
+    rank_e = rank(second_normed, r.down_e[...])
+    keep_own(r.sn_all, all_columns, second_normed)
+    keep_own(r.sn_all, ranks, rank_e)
+    to_plane(r.sn_all, r.sn_all, "sn", 0, True)
+    to_plane(r.sn_all, r.sn_all, "sn", 1, True)
+
+    def tile_at(n, width):
+        return pl.ds(pl.multiple_of(n * width, width), width)
+
+    need(5, 6)
+    from_plane(r.cot_all, "ct", 0)
+    from_plane(r.cot_all, "ct", 1)
+
+    def grad_tile(n, carry):
+        at = tile_at(n, 256)
+        r.agrad[:, at] = (
+            by_transpose(r.cot_all[:, :1024], r.wr[at, :]) + product(r.cot_all[:, 1024:], r.down_rs[:, at])
+        ).astype(BF)
+        return carry
+
+    lax.fori_loop(0, 4, grad_tile, 0)
+    for half in range(2):
+        from_plane(r.sn_all, "sn", half)
+        these = slice(half * 256, half * 256 + 256)
+
+        def inner_tile(n, carry):
+            at = tile_at(n, 256)
+            expanded = (
+                product(r.sn_all[these, :1024], r.we[:, at])
+                + r.bias_es[0:1, at]
+                + product(r.sn_all[these, 1024:], r.up_es[:, at])
+            )
+            value, slope = gelu_parts(expanded)
+            r.act[these, at] = value.astype(BF)
+            r.agrad[these, at] = (r.agrad[these, at].astype(F4) * slope).astype(BF)
+            return carry
+
+        lax.fori_loop(0, 4, inner_tile, 0)
+
+        def normed_tile(n, carry):
+            at = tile_at(n, 256)
+            r.ng_part[these, at] = by_transpose(r.agrad[these, :], r.we[at, :]).astype(BF)
+            return carry
+
+        lax.fori_loop(0, 4, normed_tile, 0)
+        r.ng_part[these, 1024:] = by_transpose(r.agrad[these, :], r.up_es[...]).astype(BF)
+        to_plane(r.ng_part, r.ng_recv, "ng", half, False)
+    def flipped(tile):
+        return tile.astype(F4).T.astype(BF)
+
+    def reduce_tile(n, carry):
+        at = tile_at(n, 256)
+        r.red_part[:, at] = product(r.act[...], r.wr[:, at]).astype(BF)
+        return carry
+
+    lax.fori_loop(0, 4, reduce_tile, 0)
+    r.red_part[:, 1024:] = by_transpose(r.act[...], r.down_rs[...]).astype(BF)
+    rank_e_t, rank_grad_r_t = flipped(r.sn_all[:, 1024:]), flipped(r.cot_all[:, 1024:])
+    for n in range(4):
+        at = slice(n * 256, (n + 1) * 256)
+        for kind, tile in enumerate((product(rank_e_t, r.agrad[:, at]), product(rank_grad_r_t, r.act[:, at]))):
+            for m in range(2):
+                to = (n * 2 + m) * 256 + kind * 128
+                r.gs[:, to : to + 128] = tile[:, m * 128 : (m + 1) * 128].astype(BF)
+    sliced = SliceReduce(l, r.gs, r.g, SLICES, (r.slice_c, r.slice_l), sems["slice"]).steps()
+    sliced.pop(0)()
+    from_plane(r.ng_recv, "ng", 0)
+    from_plane(r.ng_recv, "ng", 1)
+
+    def plane_sum(part, received, at):
+        halves = []
+        for start in (0, 256):
+            total = part[start : start + 64, at].astype(F4)
+            for j in range(1, 4):
+                total = total + received[start + j * 64 : start + j * 64 + 64, at].astype(F4)
+            halves.append(total)
+        return jnp.concatenate(halves, axis=0)
+
+    rank_grad_e = (r.sel[...] * plane_sum(r.ng_part, r.ng_recv, ranks)).astype(BF)
+    normed_grad = plane_sum(r.ng_part, r.ng_recv, all_columns) + product(rank_grad_e, r.down_e[...])
+    back_two = norm_back(r.residual[...], gain_two(), normed_grad)
+    residual_grad = r.cot[...].astype(F4) + back_two
+    mixed_grad = residual_grad.astype(BF)
+    rank_grad_m = rank(mixed_grad, r.up_m[...])
+    g_out = Exchange(l, r.send_g, r.recv_g, 64, sems["g"])
+    for step in range(4):
+        plane = lax.rem(l.z + 1 + step, 4)
+        at = pl.ds(pl.multiple_of(plane * 256, 256), 256)
+        both = by_transpose(mixed_grad, r.wm[at, :]) + product(rank_grad_m, r.down_m[:, at])
+        for n in range(2):
+            tile = both[:, n * 128 : n * 128 + 128]
+            turned = swap(tile)
+            send_g = rows_at(r.send_g, (plane * 4 + n * 2) * 64, 128)
+            send_g[0:64, :] = jnp.where(low64, tile[64:], turned[:64]).astype(BF)
+            send_g[64:128, :] = jnp.where(low64, turned[64:], tile[:64]).astype(BF)
+        for n in range(4):
+            g_out.send(plane * 4 + n)
+    g_out.own()
+
+    to_plane(r.red_part, r.red_recv, "rd", 0, False)
+    to_plane(r.red_part, r.red_recv, "rd", 1, False)
+
+    def adapter(at, left, right, width):
+        for n in range(width // 512):
+            r.gp[:, at + n * 512 : at + (n + 1) * 512] = product(left, right[:, n * 512 : (n + 1) * 512]).astype(BF)
+
+    adapter(MIXER_D, flipped(rank_grad_m), r.attended, 1024)
+    adapter(MIXER_U, flipped(rank_m), mixed_grad, 1024)
+    adapter(EXPAND_D, flipped(rank_grad_e), second_normed, 1024)
+    early = Reduce(l, r.gp, r.g, 0, TRIPLE_D, (r.early_c, r.early_1, r.early_2, r.early_3), sems["early"]).steps()
+
+    def finish_output():
+        from_plane(r.red_recv, "rd", 0)
+        from_plane(r.red_recv, "rd", 1)
+        rank_r = (r.sel[...] * plane_sum(r.red_part, r.red_recv, ranks)).astype(BF)
+        reduced = plane_sum(r.red_part, r.red_recv, all_columns)
+        r.layer_out[...] = (r.residual[...] + reduced + bias_r() + product(rank_r, r.up_r[...])).astype(BF)
+        adapter(REDUCE_U, flipped(rank_r), r.cot, 1024)
+        r.residual[...] = residual_grad
+        early.pop(0)()
+
+    for n in range(CHIPS):
+        tile = r.kv[n * 256 : n * 256 + 256, :].astype(F4)
+        wide = half_mask(256)
+        r.ones_v[n * 256 : n * 256 + 256, :] = jnp.where(wide, tile, 0.0).astype(BF)
+        r.vz[n * 256 : n * 256 + 256, :] = jnp.where(wide, 0.0, tile).astype(BF)
+        r.k_t[:, n * 256 : n * 256 + 256] = tile.T[:64, :].astype(BF)
+    r.dq_t[...] = jnp.zeros((128, 2048), F4)
+    for k in range(1, CHIPS):
+        g_out.wait(k)
+    for n in range(CHIPS):
+        at = n * 128
+        g = r.recv_g[n * 64 : n * 64 + 64, :].astype(F4)
+        both = r.attden[at : at + 128, :]
+        grad = jnp.concatenate([g, swap(g)], axis=0)
+        numer = jnp.where(low, 0.0, grad / swap(both))
+        numer_low = numer.astype(BF)
+        r.dz[at : at + 128, :] = numer_low
+        r.qd[at : at + 128, :] = jnp.where(
+            low, r.q[at : at + 128, :].astype(F4), numer_low.astype(F4)
+        ).astype(BF)
+        term = jnp.where(low, 0.0, numer * both)
+        row = -jnp.sum(term.T, axis=0, keepdims=True)
+        r.ddrow[0:1, at : at + 128] = row.astype(BF).astype(F4)
+    dkv_out = Exchange(l, r.send_dkv, r.recv_dkv, 128, sems["dkv"])
+    dq_out = Exchange(l, r.send_dq, r.recv_dq, 64, sems["dq"])
+
+    def exchange(jj):
+        for n in range(2):
+            t = 2 * jj + n
+            l.send(rows_at(r.part, t * 256 + l.o * 128, 128), rows_at(r.recv_part, t * 128, 128), sems["e"], t, (l.o, l.b))
+
+    def finish(jj):
+        for n in range(2):
+            t = 2 * jj + n
+            l.arrived(rows_at(r.recv_part, t * 128, 128), sems["e"], t)
+            here = r.part[pl.ds(pl.multiple_of(t * 256 + l.h * 128, 128), 128), :]
+            r.send_dkv[t * 128 : t * 128 + 128, :] = (here + r.recv_part[t * 128 : t * 128 + 128, :]).astype(BF)
+            y = r.dq_t[:, t * 128 : t * 128 + 128].T * 0.125
+            r.send_dq[t * 64 : t * 64 + 64, :] = jnp.where(low64, y[:64], swap(y[64:])).astype(BF)
+            dkv_out.send(t)
+            dq_out.send(t)
+
+    for jj in range(8):
+        keys = slice(jj * 512, jj * 512 + 512)
+
+        def fold_back(i, total, masked=False):
+            at = tile_at(i, 256)
+            both = r.qd[at, :]
+            powers = jnp.exp(by_transpose(r.ones_v[keys, :], both))
+            if masked:
+                row = lax.broadcasted_iota(jnp.int32, (512, 256), 0)
+                column = lax.broadcasted_iota(jnp.int32, (512, 256), 1)
+                powers = jnp.where((row < 256) | (column >= 128), powers, 0.0)
+            prob = by_transpose(r.vz[keys, :], both) + r.ddrow[0:1, at]
+            score = (powers * prob).astype(BF)
+            r.dq_t[0:64, at] += product(r.k_t[:, keys], score)
+            return total + product(score, r.q[at, :]) + product(powers.astype(BF), r.dz[at, :])
+
+        total = fold_back(jj, jnp.zeros((512, 128), F4), True)
+        if jj < 7:
+            total = lax.fori_loop(jj + 1, 8, fold_back, total)
+        r.part[keys, :] = total
+        exchange(jj)
+        if jj:
+            finish(jj - 1)
+        if jj == 2:
+            finish_output()
+        for steps in {0: [sliced], 2: [sliced], 3: [early], 4: [sliced], 5: [early], 7: [early]}.get(jj, []):
+            steps.pop(0)()
+    finish(7)
+    dkv_out.own()
+    dq_out.own()
+    for k in range(1, CHIPS):
+        dkv_out.wait(k)
+        dq_out.wait(k)
+        if k % 5 == 0:
+            early.pop(0)()
+    for p in range(8):
+        at = p * 128
+        one = r.recv_dq[p * 128 : p * 128 + 64, :].astype(F4)
+        two = r.recv_dq[p * 128 + 64 : p * 128 + 128, :].astype(F4)
+        r.jg[0:64, at : at + 128] = jnp.where(low64, one, swap(two)).astype(BF)
+        r.jg[64:128, at : at + 128] = jnp.where(low64, swap(one), two).astype(BF)
+        one = r.recv_dkv[p * 256 : p * 256 + 128, :].astype(F4)
+        two = r.recv_dkv[p * 256 + 128 : p * 256 + 256, :].astype(F4)
+        r.jg[:, 1024 + at : 1152 + at] = jnp.where(low, one, swap(two)).astype(BF)
+        r.jg[:, 2048 + at : 2176 + at] = jnp.where(low, swap(one), two).astype(BF)
+
+    rank_grad_t = rank(r.jg[...], r.up_t[...])
+    adapter(TRIPLE_D, flipped(rank_grad_t), r.fn, 1024)
+    adapter(TRIPLE_U, flipped(r.rank_t[...]), r.jg, 3072)
+    late = Reduce(l, r.gp, r.g, TRIPLE_D, SLICES - TRIPLE_D, (r.late_c, r.late_1, r.late_2, r.late_3), sems["late"]).steps()
+    late.pop(0)()
+    late.pop(0)()
+
+    def triple_tile(n, carry):
+        at = tile_at(n, 512)
+        return carry + by_transpose(r.jg[:, at], r.wt[:, at])
+
+    normed_grad = lax.fori_loop(0, 6, triple_tile, product(rank_grad_t, r.down_t[...]))
+    back_one = norm_back(r.hidden[...].astype(F4), gain_one(), normed_grad)
+    r.hidden_grad[...] = (r.residual[...] + back_one).astype(BF)
+    while late or early or sliced:
+        for rest in (late, early, sliced):
+            if rest:
+                rest.pop(0)()
+    for out in (kv_out, q_out, a_out, g_out, dkv_out, dq_out):
+        out.settle()
+    l.settle()
+
+
+def layer(*arrays):
+    vmem = pl.BlockSpec(memory_space=pltpu.VMEM)
+    hbm = pl.BlockSpec(memory_space=pl.ANY)
+    dma = pltpu.SemaphoreType.DMA
+    return pl.pallas_call(
+        layer_kernel,
+        name="layer",
+        in_specs=[hbm if name.endswith("_sh") else vmem for name in INPUTS],
+        out_shape=[jax.ShapeDtypeStruct(*OUTPUTS[name]) for name in OUTPUTS],
+        out_specs=[vmem] * len(OUTPUTS),
+        scratch_shapes=[pltpu.VMEM(*SCRATCH[name]) for name in SCRATCH]
+        + [dma((5,))]
+        + [dma(SEMS[name]) for name in SEMS for _ in range(2)],
+        compiler_params=pltpu.CompilerParams(
+            collective_id=0, has_side_effects=True, vmem_limit_bytes=LIMIT
+        ),
+    )(*arrays)
+
+
+WRITTEN = (1024, 3072, 1024, 1024, 1024, 4096, 4096, 1024)
+
+
+def write_kernel(layer_in, hidden_in, g, layer_out, hidden_out, td, tu, md, mu, ed, eu, rd, ru, low, high, in_sem, out_sem):
+    passed = [
+        pltpu.make_async_copy(layer_in, layer_out, out_sem.at[0]),
+        pltpu.make_async_copy(hidden_in, hidden_out, out_sem.at[1]),
+    ]
+    reads = [
+        pltpu.make_async_copy(
+            g.at[:, n * 2048 : (n + 1) * 2048], low.at[:, n * 2048 : (n + 1) * 2048], in_sem.at[n]
+        )
+        for n in range(8)
+    ]
+    for copy in reads + passed:
+        copy.start()
+    writes = []
+
+    def write(start, width, target, at):
+        copy = pltpu.make_async_copy(
+            high.at[:, start : start + width], target.at[:, at : at + width], out_sem.at[2 + len(writes)]
+        )
+        copy.start()
+        writes.append(copy)
+
+    whole = (
+        (MIXER_D, 1024, md, 0), (MIXER_U, 1024, mu, 0), (EXPAND_D, 1024, ed, 0), (REDUCE_U, 1024, ru, 0),
+        (TRIPLE_D, 1024, td, 0), (TRIPLE_U, 1024, tu, 0), (TRIPLE_U + 1024, 2048, tu, 1024),
+    )
+    done = 0
+    for start, width, target, at in whole:
+        while done * 2048 < start + width:
+            reads[done].wait()
+            done += 1
+        high[:, start : start + width] = low[:, start : start + width].astype(F4)
+        write(start, width, target, at)
+    for n in range(done, 8):
+        reads[n].wait()
+    for h in range(2):
+        for kind, target in enumerate((eu, rd)):
+            to = SLICES + (h * 2 + kind) * 2048
+            for z in range(4):
+                for p in range(4):
+                    source = SLICES + p * 2048 + h * 1024 + z * 256 + kind * 128
+                    here = to + (z * 4 + p) * 128
+                    high[:, here : here + 128] = low[:, source : source + 128].astype(F4)
+            write(to, 2048, target, h * 2048)
+    for copy in passed + writes:
+        copy.wait()
+
+
+def written(layer_out, hidden_grad, g):
+    hbm = pl.BlockSpec(memory_space=pl.ANY)
+    dma = pltpu.SemaphoreType.DMA
+    return pl.pallas_call(
+        write_kernel,
+        name="written",
+        in_specs=[hbm] * 3,
+        out_shape=[jax.ShapeDtypeStruct((128, 1024), BF)] * 2 + [jax.ShapeDtypeStruct((128, width), F4) for width in WRITTEN],
+        out_specs=[hbm] * 10,
+        scratch_shapes=[pltpu.VMEM((128, COLUMNS), BF), pltpu.VMEM((128, COLUMNS), F4), dma((8,)), dma((16,))],
+        compiler_params=pltpu.CompilerParams(vmem_limit_bytes=20 * 1024 * 1024),
+    )(layer_out, hidden_grad, g)
+
+
+def small_block(blocks, triple_bias, expand_bias):
+    place = lax.rem(shard_of(lax.axis_index("head"), lax.axis_index("blk")), 4)
+    lane = jnp.arange(128, dtype=jnp.int32)[None, :]
+    six = jnp.where(lane // 32 == place, jnp.tile(jnp.stack(blocks), (1, 4)), 0)
+    wide = jnp.arange(384, dtype=jnp.int32)
+    three = jnp.where(wide // 96 == place, jnp.tile(triple_bias, 4), 0).reshape(3, 128)
+    row = jnp.arange(4, dtype=jnp.int32)[:, None]
+    four = jnp.where(row == place, expand_bias[None, :], 0)
+    return jnp.concatenate([six, three, four, jnp.zeros((3, 128), BF)], axis=0).astype(BF)
+
+
+def local_fast(
+    hidden, adapter_index, first_gain, first_bias, triple_weight, triple_bias, mixer_weight, mixer_bias,
+    second_gain, second_bias, expand_weight, expand_bias, reduce_weight, reduce_bias, triple_down, triple_up,
+    mixer_down, mixer_up, expand_down, expand_up, reduce_down, reduce_up, cotangent,
+):
+    def turned(factor):
+        return jnp.transpose(factor, (0, 2, 1)).reshape(ADAPTERS * RANK, factor.shape[1])
+
+    small_sh = small_block(
+        [first_gain, first_bias, mixer_bias, second_gain, second_bias, reduce_bias], triple_bias, expand_bias
+    )
+    layer_out, hidden_grad, g = layer(
+        hidden, cotangent, selector(adapter_index), small_sh, triple_weight, mixer_weight, reduce_weight, expand_weight,
+        turned(triple_down), flat_up(triple_up), turned(mixer_down), flat_up(mixer_up),
+        turned(expand_down), flat_up(expand_up), turned(reduce_down), flat_up(reduce_up),
+    )
+    layer_out, hidden_grad, *grads = written(layer_out, hidden_grad, g)
+
+    def down_out(part):
+        return jnp.transpose(part.reshape(ADAPTERS, RANK, part.shape[1]), (0, 2, 1))
+
+    def up_out(part):
+        return part.reshape(ADAPTERS, RANK, part.shape[1])
+
+    shaped = [down_out, up_out, down_out, up_out, down_out, up_out, down_out, up_out]
+    return (layer_out, hidden_grad) + tuple(shape(part) for shape, part in zip(shaped, grads))
+
+
 def solution(mesh):
     placed = (
         P(("blk", "head"), None),
@@ -425,8 +1530,9 @@
         P(),
         P(("blk", "head"), None),
     )
+    fits = tuple(mesh.shape[name] for name in ("head", "blk")) == (2, CHIPS)
     return jax.shard_map(
-        local,
+        local_fast if fits else local,
         mesh=mesh,
         in_specs=placed,
         out_specs=(

time: 1070 us -> 263 us (0.25); the launches traced: 1060 us -> 263 us
  waiting for transfers between devices: 416 us -> 0 us
  Pallas kernels: 0 us -> 254 us
  matrix products: 181 us -> 0 us
  blocking collectives: 177 us -> 0 us
  local copies, waits for them, and re-layouts: 145 us -> 5.69 us
  loops' own time: 79.8 us -> 0 us
  other arithmetic: 42 us -> 2.74 us
  between operations: 15.6 us -> 0.88 us
    pallas_call x0 -> x2, Pallas kernels: none -> 254 us  [the longest x1 250 us: layer(): pl.pallas_call(layer_kernel, name='layer', in_specs=[hbm if name.endswith...]
    all_gather x8 -> x0, waiting for transfers between devices: 246 us -> none  [the longest x2 93.4 us: local(): lax.all_gather(payload[0], ('head', 'blk'), axis=0, tiled=True)]
    dot_general x64 -> x0, matrix products: 181 us -> none  [the longest x12 46.1 us: score_block(): jnp.einsum('qhd,khd->qhk', queries, keys_block, preferred_element_type=jn...]
    psum x1 -> x0, waiting for transfers between devices: 166 us -> none  [local(): lax.psum((triple_down_grad, triple_up_grad, mixer_down_grad, mixer_up_gra...]
    all_gather x2 -> x0, blocking collectives: 135 us -> none  [the longest x1 68.9 us: local(): lax.all_gather(payload[2], ('head', 'blk'), axis=0, tiled=True)]
    unnamed x189 -> x6, local copies, waits for them, and re-layouts: 105 us -> 4.08 us
    another operation x27 -> x0, loops' own time: 79.8 us -> none  [the longest x1 26.5 us: key_grad_fold(): return lax.scan(key_visiting, totals, shaped + (firsts,))[0]]
    unnamed x1 -> x0, blocking collectives: 41.6 us -> none
  transfers between devices with their start and end apart: 9 -> 0, of which waited for: 7 -> 0; matrix products, arithmetic and copies ran while one was open for 18% -> 0% of each run, Pallas kernels for 0% -> 0%
where the time goes in v2:
time: 263 us
  Pallas kernels  254 us (97%)
  local copies, waits for them, and re-layouts  5.69 us (2%)
  other arithmetic  2.74 us (1%)
    pallas_call x1, Pallas kernels, layer(): pl.pallas_call(layer_kernel, name='layer', in_specs=[hbm if name.endswith...  250 us

profile of v2, /device:TPU:1, one launch (start us, length us, event | category | flops | bytes accessed | tf_op | source)
XLA Modules:
  0.0 262.8 jit_solution(8274858213343053163)
XLA Ops:
  0.7 0.7 broadcast_select_fusion.1
  1.4 0.7 tile.20
  2.1 0.1 tile.21
  2.2 0.8 stack.27
  2.9 0.1 tile.9
  3.0 0.6 pad_maximum_fusion.refs_3_
  3.6 1.4 compare_convert_fusion.refs_2_
  5.0 249.6 %layer.1 = (bf16[128,1024]{1,0:T(8,128)(2,1)}, bf16[128,1024]{1,0:T(8,128)(2,1)}, bf16[128,16384]{1,0:T(8,128)(2,1)}) custom-call(bf16[128,1024]{1,0:T(8,128)(2,1)} %refs_0_.1, bf16[128,1024]{1,0:T(8,128)(2,1)} %refs_1_.1, f32[128,128]{1,0:T(8,128)} %compare_convert_fusion.refs_2_, bf16[16,128]{1,0:T(8,128)(2,1)} %pad_maximum_fusion.refs_3_, ...), custom_call_target="tpu_custom_call" | custom-call | tf_op jit(solution)/shard_map/layer/pallas_call | solution.py:1388
  254.6 0.0 copy-start
  254.6 2.2 copy-done
  256.8 0.0 copy-start.1
  256.8 0.9 copy-done.1
  257.7 0.0 copy-start.2
  257.7 0.9 copy-done.2
  258.7 4.0 %written.1 = (bf16[128,1024]{1,0:T(8,128)(2,1)}, bf16[128,1024]{1,0:T(8,128)(2,1)}, f32[128,1024]{1,0:T(8,128)}, f32[128,3072]{1,0:T(8,128)}, f32[128,1024]{1,0:...) custom-call(bf16[128,1024]{1,0:T(8,128)(2,1)S(1)} %copy-done.1, ...), custom_call_target="tpu_custom_call" | custom-call | tf_op jit(solution)/shard_map/written/pallas_call | solution.py:1457
  (7 shorter events, 0.1 us)
Async XLA Ops:
  254.6 2.2 copy-start
  256.8 0.9 copy-start.1
  257.7 0.9 copy-start.2

commit v3 on v2

--- a/solution.py
+++ b/solution.py
@@ -703,10 +703,10 @@
 
 
 class Reduce:
-    def __init__(self, links, g, out, base, width, bufs, sems):
+    def __init__(self, links, g, out, base, width, bufs, sems, rows=slice(0, 128)):
         self.l, self.g, self.out, self.base, self.sems = links, g, out, base, sems
         self.by_core, self.by_side, self.by_turn, self.by_line = bufs
-        self.half, self.p = width // 2, width // 4
+        self.half, self.p, self.rows = width // 2, width // 4, rows
         l = links
         self.mine = base + l.h * self.half
         p = self.p
@@ -716,10 +716,10 @@
         self.give2 = (self.keep1[0] + (1 - l.y) * (p // 4), self.keep1[1] + (1 - l.x) * (p // 4))
 
     def at(self, start, width):
-        return self.g.at[:, pl.ds(pl.multiple_of(start, 128), width)]
+        return self.g.at[self.rows, pl.ds(pl.multiple_of(start, 128), width)]
 
     def out_at(self, start, width):
-        return self.out.at[:, pl.ds(pl.multiple_of(start, 128), width)]
+        return self.out.at[self.rows, pl.ds(pl.multiple_of(start, 128), width)]
 
     def chunk(self, z):
         first, second = self.keep2
@@ -729,10 +729,10 @@
         tile = 384 if width % 384 == 0 else 128
         for n in range(width // tile):
             here = pl.ds(pl.multiple_of(start + n * tile, 128), tile)
-            total = self.g[:, here].astype(F4)
+            total = self.g[self.rows, here].astype(F4)
             for other in others:
                 total = total + other[:, n * tile : (n + 1) * tile].astype(F4)
-            (self.out if final else self.g)[:, here] = total.astype(BF)
+            (self.out if final else self.g)[self.rows, here] = total.astype(BF)
 
     def steps(self):
         l, p = self.l, self.p
@@ -914,12 +914,12 @@
     "recv_dkv": ((2048, 128), BF), "recv_dq": ((1024, 128), BF), "jg": ((128, 3072), BF),
 "gp": ((128, SLICES), BF), "gs": ((128, 2048), BF), "slice_c": ((128, 1024), BF), "slice_l": ((3, 128, 256), BF),
     "early_c": ((128, 2048), BF), "early_1": ((2, 128, 512), BF), "early_2": ((2, 128, 256), BF), "early_3": ((3, 128, 128), BF),
-    "late_c": ((128, 2048), BF), "late_1": ((2, 128, 512), BF), "late_2": ((2, 128, 256), BF), "late_3": ((3, 128, 128), BF),
+    "late_c": ((2, 64, 2048), BF), "late_1": ((2, 2, 64, 512), BF), "late_2": ((2, 2, 64, 256), BF), "late_3": ((2, 3, 64, 128), BF),
 }
 SEMS = {
     "z": (PIECES, 4), "x": (PIECES, 4), "y": (PIECES, 4), "d": (PIECES, 4), "c": (PIECES, 16),
     "kv": (16,), "q": (16,), "f": (16,), "a": (16,), "g": (16,), "e": (16,), "dkv": (16,), "dq": (16,),
-    "early": (16,), "late": (16,), "slice": (16,),
+    "early": (16,), "late": (16,), "late_two": (16,), "slice": (16,),
     "rz": (4,), "rc": (4,), "ep": (4,), "ez": (4, 4), "ec": (4, 4), "ct": (2, 4), "sn": (2, 4), "ng": (2, 4), "rd": (2, 4),
 }
 
@@ -977,13 +977,12 @@
     stages[2][1] += stages[5].pop(0)
     events += ordered(stages[:4], 1)
     ends = {n: len(events) for n in range(4)}
-    begun = len(events) + 1
     events += stages[4].pop(0)
+    begun = len(events)
+    events += stages[6].pop(0)
     crossed = len(events) + 8
     events += [event for stage in stages[4] for event in stage]
     ends[4] = len(events)
-    events += stages[6].pop(0)
-    kicked = len(events)
     events += [event for stage in stages[5] for event in stage]
     ends[5] = len(events)
     events += [event for stage in stages[6] for event in stage]
@@ -1089,7 +1088,6 @@
         c = l.behind(k)
         l.send(kv_at(c, l.h), kv_at(c, l.h), sems["f"], k, (l.o, l.b))
         until(min(state[0] + 1, ends[4]))
-    until(kicked)
     to_plane(r.cot_all, r.cot_all, "ct", 0, True)
     to_plane(r.cot_all, r.cot_all, "ct", 1, True)
     until(ends[5])
@@ -1335,9 +1333,9 @@
         exchange(jj)
         if jj:
             finish(jj - 1)
-        if jj == 2:
+        if jj == 1:
             finish_output()
-        for steps in {0: [sliced], 2: [sliced], 3: [early], 4: [sliced], 5: [early], 7: [early]}.get(jj, []):
+        for steps in {0: [sliced], 2: [sliced, early], 4: [early], 5: [sliced], 7: [early]}.get(jj, []):
             steps.pop(0)()
     finish(7)
     dkv_out.own()
@@ -1345,8 +1343,6 @@
     for k in range(1, CHIPS):
         dkv_out.wait(k)
         dq_out.wait(k)
-        if k % 5 == 0:
-            early.pop(0)()
     for p in range(8):
         at = p * 128
         one = r.recv_dq[p * 128 : p * 128 + 64, :].astype(F4)
@@ -1361,9 +1357,17 @@
     rank_grad_t = rank(r.jg[...], r.up_t[...])
     adapter(TRIPLE_D, flipped(rank_grad_t), r.fn, 1024)
     adapter(TRIPLE_U, flipped(r.rank_t[...]), r.jg, 3072)
-    late = Reduce(l, r.gp, r.g, TRIPLE_D, SLICES - TRIPLE_D, (r.late_c, r.late_1, r.late_2, r.late_3), sems["late"]).steps()
-    late.pop(0)()
-    late.pop(0)()
+    halves = [
+        Reduce(
+            l, r.gp, r.g, TRIPLE_D, SLICES - TRIPLE_D,
+            [buf.at[n] for buf in (r.late_c, r.late_1, r.late_2, r.late_3)],
+            sems[("late", "late_two")[n]], slice(n * 64, n * 64 + 64),
+        ).steps()
+        for n in range(2)
+    ]
+    late = [step for pair in zip(*halves) for step in pair]
+    for _ in range(4):
+        late.pop(0)()
 
     def triple_tile(n, carry):
         at = tile_at(n, 512)
@@ -1373,7 +1377,7 @@
     back_one = norm_back(r.hidden[...].astype(F4), gain_one(), normed_grad)
     r.hidden_grad[...] = (r.residual[...] + back_one).astype(BF)
     while late or early or sliced:
-        for rest in (late, early, sliced):
+        for rest in (late, late, early, sliced):
             if rest:
                 rest.pop(0)()
     for out in (kv_out, q_out, a_out, g_out, dkv_out, dq_out):

time: 263 us -> 243 us (0.924)
  Pallas kernels: 254 us -> 233 us
    pallas_call x1, Pallas kernels: 250 us -> 229 us  [layer(): pl.pallas_call(layer_kernel, name='layer', in_specs=[hbm if name.endswith...]
where the time goes in v3:
time: 243 us; the launch traced here: 242 us
  Pallas kernels  233 us (96%)
  local copies, waits for them, and re-layouts  5.69 us (2%)
  other arithmetic  2.74 us (1%)
    pallas_call x1, Pallas kernels, layer(): pl.pallas_call(layer_kernel, name='layer', in_specs=[hbm if name.endswith...  229 us

profile of v3, /device:TPU:1, one launch (start us, length us, event | category | flops | bytes accessed | tf_op | source)
XLA Modules:
  0.0 242.3 jit_solution(10279161147031800515)
XLA Ops:
  0.7 0.7 broadcast_select_fusion.1
  1.4 0.7 tile.20
  2.1 0.1 tile.21
  2.2 0.8 stack.27
  2.9 0.1 tile.9
  3.0 0.6 pad_maximum_fusion.refs_3_
  3.6 1.4 compare_convert_fusion.refs_2_
  5.0 229.1 %layer.1 = (bf16[128,1024]{1,0:T(8,128)(2,1)}, bf16[128,1024]{1,0:T(8,128)(2,1)}, bf16[128,16384]{1,0:T(8,128)(2,1)}) custom-call(bf16[128,1024]{1,0:T(8,128)(2,1)} %refs_0_.1, bf16[128,1024]{1,0:T(8,128)(2,1)} %refs_1_.1, f32[128,128]{1,0:T(8,128)} %compare_convert_fusion.refs_2_, bf16[16,128]{1,0:T(8,128)(2,1)} %pad_maximum_fusion.refs_3_, ...), custom_call_target="tpu_custom_call" | custom-call | tf_op jit(solution)/shard_map/layer/pallas_call | solution.py:1392
  234.1 0.0 copy-start
  234.1 2.2 copy-done
  236.3 0.0 copy-start.1
  236.3 0.9 copy-done.1
  237.2 0.0 copy-start.2
  237.2 0.9 copy-done.2
  238.2 4.0 %written.1 = (bf16[128,1024]{1,0:T(8,128)(2,1)}, bf16[128,1024]{1,0:T(8,128)(2,1)}, f32[128,1024]{1,0:T(8,128)}, f32[128,3072]{1,0:T(8,128)}, f32[128,1024]{1,0:...) custom-call(bf16[128,1024]{1,0:T(8,128)(2,1)S(1)} %copy-done.1, ...), custom_call_target="tpu_custom_call" | custom-call | tf_op jit(solution)/shard_map/written/pallas_call | solution.py:1461
  (7 shorter events, 0.1 us)
Async XLA Ops:
  234.1 2.2 copy-start
  236.3 0.9 copy-start.1
  237.2 0.9 copy-start.2

commit v4 on v3

--- a/solution.py
+++ b/solution.py
@@ -1305,12 +1305,17 @@
             l.arrived(rows_at(r.recv_part, t * 128, 128), sems["e"], t)
             here = r.part[pl.ds(pl.multiple_of(t * 256 + l.h * 128, 128), 128), :]
             r.send_dkv[t * 128 : t * 128 + 128, :] = (here + r.recv_part[t * 128 : t * 128 + 128, :]).astype(BF)
+            dkv_out.send(t)
+
+    def finish_queries(i):
+        for t in (2 * i, 2 * i + 1):
             y = r.dq_t[:, t * 128 : t * 128 + 128].T * 0.125
             r.send_dq[t * 64 : t * 64 + 64, :] = jnp.where(low64, y[:64], swap(y[64:])).astype(BF)
-            dkv_out.send(t)
             dq_out.send(t)
 
-    for jj in range(8):
+    order = (4, 0, 5, 1, 6, 2, 7, 3)
+    queries_sent = 0
+    for place, jj in enumerate(order):
         keys = slice(jj * 512, jj * 512 + 512)
 
         def fold_back(i, total, masked=False):
@@ -1331,13 +1336,16 @@
             total = lax.fori_loop(jj + 1, 8, fold_back, total)
         r.part[keys, :] = total
         exchange(jj)
-        if jj:
-            finish(jj - 1)
-        if jj == 1:
+        if place:
+            finish(order[place - 1])
+        while queries_sent < 8 and all(n in order[: place + 1] for n in range(queries_sent + 1)):
+            finish_queries(queries_sent)
+            queries_sent += 1
+        if place == 1:
             finish_output()
-        for steps in {0: [sliced], 2: [sliced, early], 4: [early], 5: [sliced], 7: [early]}.get(jj, []):
+        for steps in {0: [sliced], 2: [sliced, early], 4: [early], 5: [sliced], 7: [early]}.get(place, []):
             steps.pop(0)()
-    finish(7)
+    finish(order[-1])
     dkv_out.own()
     dq_out.own()
     for k in range(1, CHIPS):

time: 243 us -> 236 us (0.971)
  Pallas kernels: 233 us -> 226 us
    pallas_call x1, Pallas kernels: 229 us -> 222 us  [layer(): pl.pallas_call(layer_kernel, name='layer', in_specs=[hbm if name.endswith...]
where the time goes in v4:
time: 236 us; the launch traced here: 235 us
  Pallas kernels  226 us (96%)
  local copies, waits for them, and re-layouts  5.69 us (2%)
  other arithmetic  2.74 us (1%)
    pallas_call x1, Pallas kernels, layer(): pl.pallas_call(layer_kernel, name='layer', in_specs=[hbm if name.endswith...  222 us

profile of v4, /device:TPU:1, one launch (start us, length us, event | category | flops | bytes accessed | tf_op | source)
XLA Modules:
  0.0 235.3 jit_solution(23420619728951321)
XLA Ops:
  0.7 0.7 broadcast_select_fusion.1
  1.4 0.7 tile.20
  2.1 0.1 tile.21
  2.2 0.8 stack.27
  2.9 0.1 tile.9
  3.0 0.6 pad_maximum_fusion.refs_3_
  3.6 1.4 compare_convert_fusion.refs_2_
  5.0 222.0 %layer.1 = (bf16[128,1024]{1,0:T(8,128)(2,1)}, bf16[128,1024]{1,0:T(8,128)(2,1)}, bf16[128,16384]{1,0:T(8,128)(2,1)}) custom-call(bf16[128,1024]{1,0:T(8,128)(2,1)} %refs_0_.1, bf16[128,1024]{1,0:T(8,128)(2,1)} %refs_1_.1, f32[128,128]{1,0:T(8,128)} %compare_convert_fusion.refs_2_, bf16[16,128]{1,0:T(8,128)(2,1)} %pad_maximum_fusion.refs_3_, ...), custom_call_target="tpu_custom_call" | custom-call | tf_op jit(solution)/shard_map/layer/pallas_call | solution.py:1400
  227.0 0.0 copy-start
  227.0 2.2 copy-done
  229.2 0.0 copy-start.1
  229.2 0.9 copy-done.1
  230.2 0.0 copy-start.2
  230.2 0.9 copy-done.2
  231.1 4.0 %written.1 = (bf16[128,1024]{1,0:T(8,128)(2,1)}, bf16[128,1024]{1,0:T(8,128)(2,1)}, f32[128,1024]{1,0:T(8,128)}, f32[128,3072]{1,0:T(8,128)}, f32[128,1024]{1,0:...) custom-call(bf16[128,1024]{1,0:T(8,128)(2,1)S(1)} %copy-done.1, ...), custom_call_target="tpu_custom_call" | custom-call | tf_op jit(solution)/shard_map/written/pallas_call | solution.py:1469
  (7 shorter events, 0.1 us)
Async XLA Ops:
  227.0 2.2 copy-start
  229.2 0.9 copy-start.1
  230.2 0.9 copy-start.2

commit v5 on v4

--- a/solution.py
+++ b/solution.py
@@ -892,14 +892,14 @@
 )
 
 INPUTS = (
-    "hidden", "cot", "sel", "small_sh", "triple_sh", "mixer_sh", "reduce_sh", "expand_sh",
+    "hidden", "cot", "index", "small_sh", "triple_sh", "mixer_sh", "reduce_sh", "expand_sh",
     "down_t", "up_t", "down_m", "up_m", "down_e", "up_e", "down_r", "up_r",
 )
 OUTPUTS = {"layer_out": ((128, 1024), BF), "hidden_grad": ((128, 1024), BF), "g": ((128, COLUMNS), BF)}
 SCRATCH = {
     "wt": ((1024, 3072), BF), "wm": ((1024, 1024), BF), "wr": ((1024, 1024), BF), "we": ((1024, 1024), BF),
     "e_in": ((32, 4096), BF), "e_stage": ((128, 1024), BF), "up_es": ((128, 1024), BF), "down_rs": ((128, 1024), BF), "bias_es": ((1, 1024), F4),
-    "small": ((512, 128), BF), "vecs": ((16, 1024), F4), "bias_t": ((1, 3072), F4), "bias_e": ((1, 4096), F4),
+    "sel": ((128, 128), F4), "small": ((512, 128), BF), "vecs": ((16, 1024), F4), "bias_t": ((1, 3072), F4), "bias_e": ((1, 4096), F4),
     "fn": ((128, 1024), BF), "rank_t": ((128, 128), BF), "kv": ((4096, 128), BF), "q": ((2048, 128), BF),
     "attden": ((2048, 128), F4), "attended": ((128, 1024), BF), "ones_v": ((4096, 128), BF),
     "send_kv": ((2048, 128), BF), "send_q": ((1024, 128), BF), "recv_q": ((1024, 128), BF),
@@ -943,6 +943,8 @@
     for copy in local_copies:
         copy.start()
     l.greet()
+    adapter_of = lax.broadcasted_iota(jnp.int32, (128, 128), 0) // RANK
+    r.sel[...] = jnp.where(adapter_of == r.index[...], 1.0, 0.0).T
 
     def columns(ref, at):
         return lambda h, chip: ref.at[
@@ -1103,7 +1105,7 @@
         tile = r.kv[n * 256 : n * 256 + 256, :].astype(F4)
         r.ones_v[n * 256 : n * 256 + 256, :] = jnp.where(half_mask(256), 1.0, tile).astype(BF)
     a_out = Exchange(l, r.send_a, r.recv_a, 64, sems["a"])
-    for i in range(8):
+    for i in (7, 0, 6, 1, 5, 2, 4, 3):
         queries = r.q[i * 256 : (i + 1) * 256, :]
 
         def fold(jj, total, masked=False):
@@ -1500,7 +1502,7 @@
         [first_gain, first_bias, mixer_bias, second_gain, second_bias, reduce_bias], triple_bias, expand_bias
     )
     layer_out, hidden_grad, g = layer(
-        hidden, cotangent, selector(adapter_index), small_sh, triple_weight, mixer_weight, reduce_weight, expand_weight,
+        hidden, cotangent, adapter_index.reshape(1, 128), small_sh, triple_weight, mixer_weight, reduce_weight, expand_weight,
         turned(triple_down), flat_up(triple_up), turned(mixer_down), flat_up(mixer_up),
         turned(expand_down), flat_up(expand_up), turned(reduce_down), flat_up(reduce_up),
     )

time: 236 us -> 234 us (level)
  no operation moved by 1% of the time
where the time goes in v5:
time: 234 us; the launch traced here: 233 us
  Pallas kernels  225 us (96%)
  local copies, waits for them, and re-layouts  5.69 us (2%)
    pallas_call x1, Pallas kernels, layer(): pl.pallas_call(layer_kernel, name='layer', in_specs=[hbm if name.endswith...  222 us

profile of v5, /device:TPU:1, one launch (start us, length us, event | category | flops | bytes accessed | tf_op | source)
XLA Modules:
  0.0 233.4 jit_solution(420147233603140123)
XLA Ops:
  0.7 0.7 broadcast_select_fusion.1
  1.4 0.7 tile.20
  2.1 0.1 tile.21
  2.2 0.8 stack.27
  2.9 0.1 tile.9
  3.0 0.6 pad_maximum_fusion.refs_3_
  3.6 221.5 %layer.1 = (bf16[128,1024]{1,0:T(8,128)(2,1)}, bf16[128,1024]{1,0:T(8,128)(2,1)}, bf16[128,16384]{1,0:T(8,128)(2,1)}) custom-call(bf16[128,1024]{1,0:T(8,128)(2,1)} %refs_0_.1, bf16[128,1024]{1,0:T(8,128)(2,1)} %refs_1_.1, s32[1,128]{1,0:T(1,128)} %bitcast.47, bf16[16,128]{1,0:T(8,128)(2,1)} %pad_maximum_fusion.refs_3_, bf16[32,3072]{1,0:T(8,128)(2,1)} %refs_4_.1, ...), custom_call_target="tpu_custom_call" | custom-call | tf_op jit(solution)/shard_map/layer/pallas_call | solution.py:1402
  225.2 0.0 copy-start
  225.2 2.2 copy-done
  227.3 0.0 copy-start.1
  227.3 0.9 copy-done.1
  228.3 0.0 copy-start.2
  228.3 0.9 copy-done.2
  229.2 4.0 %written.1 = (bf16[128,1024]{1,0:T(8,128)(2,1)}, bf16[128,1024]{1,0:T(8,128)(2,1)}, f32[128,1024]{1,0:T(8,128)}, f32[128,3072]{1,0:T(8,128)}, f32[128,1024]{1,0:...) custom-call(bf16[128,1024]{1,0:T(8,128)(2,1)S(1)} %copy-done.1, ...), custom_call_target="tpu_custom_call" | custom-call | tf_op jit(solution)/shard_map/written/pallas_call | solution.py:1471
  (6 shorter events, 0.0 us)
Async XLA Ops:
  225.2 2.2 copy-start
  227.3 0.9 copy-start.1
  228.3 0.9 copy-start.2

commit v6 on v5

--- a/solution.py
+++ b/solution.py
@@ -1353,6 +1353,8 @@
     for k in range(1, CHIPS):
         dkv_out.wait(k)
         dq_out.wait(k)
+    early.pop(0)()
+    sliced.pop(0)()
     for p in range(8):
         at = p * 128
         one = r.recv_dq[p * 128 : p * 128 + 64, :].astype(F4)

time: 234 us -> 234 us (level)
  no operation moved by 1% of the time
where the time goes in v6:
time: 234 us
  Pallas kernels  226 us (97%)
  local copies, waits for them, and re-layouts  5.69 us (2%)
    pallas_call x1, Pallas kernels, layer(): pl.pallas_call(layer_kernel, name='layer', in_specs=[hbm if name.endswith...  222 us

profile of v6, /device:TPU:1, one launch (start us, length us, event | category | flops | bytes accessed | tf_op | source)
XLA Modules:
  0.0 234.2 jit_solution(10756183475427331176)
XLA Ops:
  0.7 0.7 broadcast_select_fusion.1
  1.4 0.7 tile.20
  2.1 0.1 tile.21
  2.2 0.8 stack.27
  2.9 0.1 tile.9
  3.0 0.6 pad_maximum_fusion.refs_3_
  3.6 222.3 %layer.1 = (bf16[128,1024]{1,0:T(8,128)(2,1)}, bf16[128,1024]{1,0:T(8,128)(2,1)}, bf16[128,16384]{1,0:T(8,128)(2,1)}) custom-call(bf16[128,1024]{1,0:T(8,128)(2,1)} %refs_0_.1, bf16[128,1024]{1,0:T(8,128)(2,1)} %refs_1_.1, s32[1,128]{1,0:T(1,128)} %bitcast.47, bf16[16,128]{1,0:T(8,128)(2,1)} %pad_maximum_fusion.refs_3_, bf16[32,3072]{1,0:T(8,128)(2,1)} %refs_4_.1, ...), custom_call_target="tpu_custom_call" | custom-call | tf_op jit(solution)/shard_map/layer/pallas_call | solution.py:1404
  225.9 0.0 copy-start
  226.0 2.2 copy-done
  228.1 0.0 copy-start.1
  228.1 0.9 copy-done.1
  229.1 0.0 copy-start.2
  229.1 0.9 copy-done.2
  230.0 4.0 %written.1 = (bf16[128,1024]{1,0:T(8,128)(2,1)}, bf16[128,1024]{1,0:T(8,128)(2,1)}, f32[128,1024]{1,0:T(8,128)}, f32[128,3072]{1,0:T(8,128)}, f32[128,1024]{1,0:...) custom-call(bf16[128,1024]{1,0:T(8,128)(2,1)S(1)} %copy-done.1, ...), custom_call_target="tpu_custom_call" | custom-call | tf_op jit(solution)/shard_map/written/pallas_call | solution.py:1473
  (6 shorter events, 0.0 us)
Async XLA Ops:
  225.9 2.2 copy-start
  228.1 0.9 copy-start.1
  229.1 0.9 copy-start.2
